TPU v7x, 32 devices: a whole 2x2x4 slice. The times are simulated.
32 devices in a mesh: dp: 8 (over z, x), pipe: 4 (over y, core).
Axes of the slice: x: 2, y: 2, z: 4, core: 2. Of those that a mesh axis runs over, the one named last changes fastest.
Arguments:
- images: bfloat16 [64, 196, 768], P('dp'), may hold values from -6 to 6
- cotangent: bfloat16 [64, 196, 768], P('dp'), may hold values from -6 to 6
- valid_rows: int32 [64], P('dp'), may hold values from 0 to 1, as said below
- skip_masks: int32 [64, 2], P('dp'), may hold values 0 or 1
- norm_gain: bfloat16 [4, 768], P('pipe'), may hold values from 0.5 to 1.5
- norm_bias: bfloat16 [4, 768], P('pipe'), may hold values from -3 to 3
- token_up: bfloat16 [392, 384], P('pipe'), may hold values from -0.4375 to 0.4375
- token_up_bias: bfloat16 [768], P('pipe'), may hold values from -3 to 3
- token_down: bfloat16 [768, 196], P('pipe'), may hold values from -0.3125 to 0.3125
- token_down_bias: bfloat16 [392], P('pipe'), may hold values from -3 to 3
- chan_up: bfloat16 [1536, 3072], P('pipe'), may hold values from -0.21875 to 0.21875
- chan_up_bias: bfloat16 [6144], P('pipe'), may hold values from -3 to 3
- chan_down: bfloat16 [6144, 768], P('pipe'), may hold values from -0.109375 to 0.109375
- chan_down_bias: bfloat16 [1536], P('pipe'), may hold values from -3 to 3
Outputs:
- mixed: bfloat16 [64, 196, 768], P('dp', None, 'pipe')
- input_grad: bfloat16 [64, 196, 768], P('dp', None, 'pipe')
- norm_gain_grad: float32 [4, 768], P('pipe')
- norm_bias_grad: float32 [4, 768], P('pipe')
- token_up_grad: float32 [392, 384], P('pipe')
- token_up_bias_grad: float32 [768], P('pipe')
- token_down_grad: float32 [768, 196], P('pipe')
- token_down_bias_grad: float32 [392], P('pipe')
- chan_up_grad: float32 [1536, 3072], P('pipe', 'dp')
- chan_up_bias_grad: float32 [6144], P('pipe')
- chan_down_grad: float32 [6144, 768], P('pipe', 'dp')
- chan_down_bias_grad: float32 [1536], P('pipe')
Inputs may be any that keep to these rules, and one draw needn't show every extreme that they name: `valid_rows`: each block of 8 consecutive slots (one index of dp) holds 4 or more valid images; in every draw some block has all 8 valid.
All inputs are finite; a program needn't handle non-finite values. No bound on the sum of `skip_masks` on one device may be relied on, other than what follows from the above.
Results may differ from a plain program's by a relative error of at most 0.013.
Values may be sent and summed in bfloat16 or wider, within the bound.
No kernel may reach another device: no remote copies, remote signals or barrier semaphores. Data moves between devices by JAX's collectives and lax.ppermute only.
A program may use at most 256 MiB of HBM per device.

v0:
```python
import jax
import jax.numpy as jnp
from jax import lax
from jax.sharding import PartitionSpec as P

MICRO = 2


NORM_EPS = 1e-06


def swapped(block, axis, distance):
    count = lax.axis_size(axis)
    route = []
    for low in range(count):
        high = low | 1 << distance
        if high != low and high < count:
            route += [(low, high), (high, low)]
    return lax.ppermute(block, axis, route)


def from_behind(x, axis, by):
    size = lax.axis_size(axis)
    pairs = [(i, i + by) for i in range(size) if 0 <= i + by < size]
    return lax.ppermute(x, axis, pairs)


def as_sent(x):

    def short(part):
        return part.astype(jnp.bfloat16) if part.dtype == jnp.float32 else part

    return jax.tree.map(short, x)


def norm_rows(hidden, gain_row, shift_row):
    row_mean = jnp.mean(hidden, axis=-1, keepdims=True)
    centred = hidden - row_mean
    row_scale = lax.rsqrt(jnp.mean(centred * centred, axis=-1, keepdims=True) + NORM_EPS)
    return centred * row_scale * gain_row + shift_row


def gelu_tanh(values_in):
    return jax.nn.gelu(values_in, approximate=True)


def token_pre(normed, weights):
    product = jnp.einsum("bpd,pt->bdt", normed, weights[0], preferred_element_type=jnp.float32)
    return product + weights[1].astype(jnp.float32)


def token_out(pre_act, weights):
    activated = gelu_tanh(pre_act).astype(jnp.bfloat16)
    product = jnp.einsum("bdt,tp->bpd", activated, weights[2], preferred_element_type=jnp.float32)
    return product + weights[3].astype(jnp.float32)[None, :, None]


def chan_pre(normed, weights):
    product = jnp.einsum("bpd,df->bpf", normed, weights[0], preferred_element_type=jnp.float32)
    return product + weights[1].astype(jnp.float32)


def chan_out(pre_act, weights):
    activated = gelu_tanh(pre_act).astype(jnp.bfloat16)
    product = jnp.einsum("bpf,fd->bpd", activated, weights[2], preferred_element_type=jnp.float32)
    return product + weights[3].astype(jnp.float32)


def token_back(hidden, saved_pre, grad_out, rows_mask, gain_row, shift_row, weights):
    normed_full, norm_pull = jax.vjp(norm_rows, hidden, gain_row, shift_row)
    normed = normed_full.astype(jnp.bfloat16)
    pre_act = token_pre(normed, weights) if saved_pre is None else saved_pre
    activated = gelu_tanh(pre_act).astype(jnp.bfloat16)
    grad_branch = (rows_mask[:, None, None] * grad_out).astype(jnp.bfloat16)
    grad_w_down = jnp.einsum(
        "bdt,bpd->tp", activated, grad_branch, preferred_element_type=jnp.float32
    )
    grad_bias_down = jnp.sum(grad_branch, axis=(0, 2), dtype=jnp.float32)
    grad_act = jnp.einsum(
        "bpd,tp->bdt", grad_branch, weights[2], preferred_element_type=jnp.float32
    )
    gelu_pull = jax.vjp(gelu_tanh, pre_act)[1]
    grad_pre = gelu_pull(grad_act)[0].astype(jnp.bfloat16)
    grad_w_up = jnp.einsum("bpd,bdt->pt", normed, grad_pre, preferred_element_type=jnp.float32)
    grad_bias_up = jnp.sum(grad_pre, axis=(0, 1), dtype=jnp.float32)
    grad_normed = jnp.einsum(
        "bdt,pt->bpd", grad_pre, weights[0], preferred_element_type=jnp.float32
    )
    grad_hidden, grad_gain, grad_shift = norm_pull(grad_normed)
    return (
        grad_out + grad_hidden,
        (grad_gain, grad_shift, grad_w_up, grad_bias_up, grad_w_down, grad_bias_down),
    )


def chan_back(hidden, saved_pre, grad_out, rows_mask, gain_row, shift_row, weights):
    normed_full, norm_pull = jax.vjp(norm_rows, hidden, gain_row, shift_row)
    normed = normed_full.astype(jnp.bfloat16)
    pre_act = chan_pre(normed, weights) if saved_pre is None else saved_pre
    activated = gelu_tanh(pre_act).astype(jnp.bfloat16)
    grad_branch = (rows_mask[:, None, None] * grad_out).astype(jnp.bfloat16)
    grad_w_down = jnp.einsum(
        "bpf,bpd->fd", activated, grad_branch, preferred_element_type=jnp.float32
    )
    grad_bias_down = jnp.sum(grad_branch, axis=(0, 1), dtype=jnp.float32)
    grad_act = jnp.einsum(
        "bpd,fd->bpf", grad_branch, weights[2], preferred_element_type=jnp.float32
    )
    gelu_pull = jax.vjp(gelu_tanh, pre_act)[1]
    grad_pre = gelu_pull(grad_act)[0].astype(jnp.bfloat16)
    grad_w_up = jnp.einsum("bpd,bpf->df", normed, grad_pre, preferred_element_type=jnp.float32)
    grad_bias_up = jnp.sum(grad_pre, axis=(0, 1), dtype=jnp.float32)
    grad_normed = jnp.einsum(
        "bpf,df->bpd", grad_pre, weights[0], preferred_element_type=jnp.float32
    )
    grad_hidden, grad_gain, grad_shift = norm_pull(grad_normed)
    return (
        grad_out + grad_hidden,
        (grad_gain, grad_shift, grad_w_up, grad_bias_up, grad_w_down, grad_bias_down),
    )


def store_slot(buffer, new_value, slot_index, is_live):
    current = lax.dynamic_index_in_dim(buffer, slot_index, 0, keepdims=False)
    chosen = jnp.where(is_live, new_value, current)
    return lax.dynamic_update_index_in_dim(buffer, chosen, slot_index, 0)


def local(
    images,
    cotangent,
    valid_rows,
    skip_masks,
    norm_gain,
    norm_bias,
    token_up,
    token_up_bias,
    token_down,
    token_down_bias,
    chan_up,
    chan_up_bias,
    chan_down,
    chan_down_bias,
):
    pipe_size = lax.axis_size("pipe")
    section_index = lax.axis_index("pipe")
    section_kind = section_index % 2
    layer_index = section_index // 2
    leading = section_kind == 0
    last_section = pipe_size - 1
    slot_count = images.shape[0]
    patches = images.shape[1]
    feature_count = images.shape[2]
    per_micro = slot_count // MICRO
    token_width = token_up.shape[1]
    chan_width = chan_up.shape[1]
    gain_row = norm_gain[0].astype(jnp.float32)
    shift_row = norm_bias[0].astype(jnp.float32)
    own_parts = (
        token_up,
        token_up_bias,
        token_down,
        token_down_bias,
        chan_up,
        chan_up_bias,
        chan_down,
        chan_down_bias,
    )
    partner_parts = swapped(
        (
            token_up,
            token_up_bias,
            token_down,
            token_down_bias,
            chan_up,
            chan_up_bias,
            chan_down,
            chan_down_bias,
        ),
        "pipe",
        0,
    )

    def join_halves(mine_part, their_part):
        return jnp.where(
            leading,
            jnp.concatenate([mine_part, their_part], 0),
            jnp.concatenate([their_part, mine_part], 0),
        )

    full_parts = [
        join_halves(mine_part, their_part)
        for mine_part, their_part in zip(own_parts, partner_parts)
    ]
    token_weights = tuple(full_parts[:4])
    chan_weights = tuple(full_parts[4:])
    skip_layer = jnp.where(layer_index == 0, skip_masks[:, 0], skip_masks[:, 1]).astype(jnp.float32)
    valid_float = valid_rows.astype(jnp.float32)
    token_shape = (per_micro, feature_count, token_width)
    chan_shape = (per_micro, patches, chan_width)

    def spare_forward(hidden, rows_mask):
        return (
            jnp.zeros_like(hidden),
            jnp.zeros(token_shape, jnp.float32),
            jnp.zeros(chan_shape, jnp.float32),
        )

    def token_forward(hidden, rows_mask):
        normed = norm_rows(hidden, gain_row, shift_row).astype(jnp.bfloat16)
        pre_act = token_pre(normed, token_weights)
        result = hidden + rows_mask[:, None, None] * token_out(pre_act, token_weights)
        return (result, pre_act, jnp.zeros(chan_shape, jnp.float32))

    def chan_forward(hidden, rows_mask):
        normed = norm_rows(hidden, gain_row, shift_row).astype(jnp.bfloat16)
        pre_act = chan_pre(normed, chan_weights)
        result = hidden + rows_mask[:, None, None] * chan_out(pre_act, chan_weights)
        return (result, jnp.zeros(token_shape, jnp.float32), pre_act)

    tick_count = MICRO + pipe_size - 1
    incoming = jnp.zeros((per_micro, patches, feature_count), jnp.bfloat16)
    kept_inputs = jnp.zeros((MICRO, per_micro, patches, feature_count), jnp.bfloat16)
    finals = jnp.zeros((MICRO, per_micro, patches, feature_count), jnp.bfloat16)
    kept_token = jnp.zeros((MICRO,) + token_shape, jnp.float32)
    kept_chan = jnp.zeros((MICRO,) + chan_shape, jnp.float32)
    for tick_index in range(tick_count):
        micro_index = tick_index - section_index
        is_live = (micro_index >= 0) & (micro_index < MICRO)
        slot_index = jnp.clip(micro_index, 0, MICRO - 1)
        row_start = slot_index * per_micro
        fresh_rows = lax.dynamic_slice_in_dim(images, row_start, per_micro, 0)
        section_in = jnp.where(section_index == 0, fresh_rows, incoming)
        rows_mask = lax.dynamic_slice_in_dim(skip_layer, row_start, per_micro, 0)
        branch_pick = jnp.where(is_live, 1 + section_kind, 0)
        result = lax.switch(
            branch_pick,
            [spare_forward, token_forward, chan_forward],
            section_in.astype(jnp.float32),
            rows_mask,
        )
        sent_rows = result[0].astype(jnp.bfloat16)
        kept_inputs = store_slot(kept_inputs, section_in, slot_index, is_live)
        finals = store_slot(finals, sent_rows, slot_index, is_live)
        kept_token = store_slot(kept_token, result[1], slot_index, is_live)
        kept_chan = store_slot(kept_chan, result[2], slot_index, is_live)
        if tick_index + 1 < tick_count:
            incoming = from_behind(sent_rows, "pipe", 1)

    def spare_backward(hidden, saved, grad_out, rows_mask, grad_totals):
        return (jnp.zeros_like(grad_out), grad_totals)

    def token_backward(hidden, saved, grad_out, rows_mask, grad_totals):
        saved_pre = saved[0]
        grad_in, added = token_back(
            hidden, saved_pre, grad_out, rows_mask, gain_row, shift_row, token_weights
        )
        updated = tuple((old_part + new_part for old_part, new_part in zip(grad_totals[:6], added)))
        return (grad_in, updated + grad_totals[6:])

    def chan_backward(hidden, saved, grad_out, rows_mask, grad_totals):
        saved_pre = saved[1]
        grad_in, added = chan_back(
            hidden, saved_pre, grad_out, rows_mask, gain_row, shift_row, chan_weights
        )
        norm_part = (grad_totals[0] + added[0], grad_totals[1] + added[1])
        chan_part = tuple(
            (old_part + new_part for old_part, new_part in zip(grad_totals[6:], added[2:]))
        )
        return (grad_in, norm_part + grad_totals[2:6] + chan_part)

    grad_totals = tuple(
        (
            jnp.zeros(array.shape, jnp.float32)
            for array in (gain_row, shift_row) + token_weights + chan_weights
        )
    )
    incoming_grad = jnp.zeros((per_micro, patches, feature_count), jnp.bfloat16)
    input_grads = jnp.zeros((MICRO, per_micro, patches, feature_count), jnp.bfloat16)
    for tick_index in range(tick_count):
        micro_index = tick_index - (last_section - section_index)
        is_live = (micro_index >= 0) & (micro_index < MICRO)
        slot_index = jnp.clip(micro_index, 0, MICRO - 1)
        row_start = slot_index * per_micro
        seed_rows = lax.dynamic_slice_in_dim(cotangent, row_start, per_micro, 0).astype(jnp.float32)
        seed_valid = lax.dynamic_slice_in_dim(valid_float, row_start, per_micro, 0)
        grad_out = jnp.where(
            section_index == last_section,
            seed_rows * seed_valid[:, None, None],
            incoming_grad.astype(jnp.float32),
        )
        hidden = lax.dynamic_index_in_dim(kept_inputs, slot_index, 0, keepdims=False).astype(
            jnp.float32
        )
        rows_mask = lax.dynamic_slice_in_dim(skip_layer, row_start, per_micro, 0)
        saved = (
            lax.dynamic_index_in_dim(kept_token, slot_index, 0, keepdims=False),
            lax.dynamic_index_in_dim(kept_chan, slot_index, 0, keepdims=False),
        )
        branch_pick = jnp.where(is_live, 1 + section_kind, 0)
        grad_in, grad_totals = lax.switch(
            branch_pick,
            [spare_backward, token_backward, chan_backward],
            hidden,
            saved,
            grad_out,
            rows_mask,
            grad_totals,
        )
        sent_grad = grad_in.astype(jnp.bfloat16)
        input_grads = store_slot(input_grads, sent_grad, slot_index, is_live)
        if tick_index + 1 < tick_count:
            incoming_grad = from_behind(sent_grad, "pipe", -1)
    final_rows = finals.reshape(slot_count, patches, feature_count)
    valid_low = valid_rows.astype(jnp.bfloat16)[:, None, None]
    zero_low = jnp.zeros((), jnp.bfloat16)
    mixed_term = jnp.where(section_index == last_section, final_rows * valid_low, zero_low)
    grad_rows = input_grads.reshape(slot_count, patches, feature_count)
    grad_term = jnp.where(section_index == 0, grad_rows, zero_low)
    mixed_sum, grad_sum = (
        lax.psum_scatter(mixed_term, "pipe", scatter_dimension=2, tiled=True).astype(jnp.float32),
        lax.psum_scatter(grad_term, "pipe", scatter_dimension=2, tiled=True).astype(jnp.float32),
    )
    mixed = mixed_sum.astype(jnp.bfloat16)
    input_grad = grad_sum.astype(jnp.bfloat16)

    def split_halves(array):
        half_rows = array.shape[0] // 2
        upper = array[:half_rows]
        lower = array[half_rows:]
        return (jnp.where(leading, upper, lower), jnp.where(leading, lower, upper))

    pairs = [split_halves(array) for array in grad_totals[2:]]
    mine_parts = [pair[0] for pair in pairs]
    their_parts = [pair[1] for pair in pairs]
    received = swapped(
        (
            as_sent(their_parts[0]),
            as_sent(their_parts[1]),
            as_sent(their_parts[2]),
            as_sent(their_parts[3]),
            as_sent(their_parts[4]),
            as_sent(their_parts[5]),
            as_sent(their_parts[6]),
            as_sent(their_parts[7]),
        ),
        "pipe",
        0,
    )
    joined = [mine_part + got_part for mine_part, got_part in zip(mine_parts, received)]
    up_sum, down_sum = (
        lax.psum_scatter(joined[4], "dp", scatter_dimension=1, tiled=True),
        lax.psum_scatter(joined[6], "dp", scatter_dimension=1, tiled=True),
    )
    summed = lax.psum(
        (
            grad_totals[0],
            grad_totals[1],
            joined[0],
            joined[1],
            joined[2],
            joined[3],
            joined[5],
            joined[7],
        ),
        "dp",
    )
    final_parts = [
        summed[2],
        summed[3],
        summed[4],
        summed[5],
        up_sum,
        summed[6],
        down_sum,
        summed[7],
    ]
    gain_sum = summed[0]
    shift_sum = summed[1]
    return (
        mixed,
        input_grad,
        gain_sum[None, :],
        shift_sum[None, :],
        final_parts[0],
        final_parts[1],
        final_parts[2],
        final_parts[3],
        final_parts[4],
        final_parts[5],
        final_parts[6],
        final_parts[7],
    )


def solution(mesh):
    placed = (
        P("dp", None, None),
        P("dp", None, None),
        P("dp"),
        P("dp", None),
        P("pipe", None),
        P("pipe", None),
        P("pipe", None),
        P("pipe"),
        P("pipe", None),
        P("pipe"),
        P("pipe", None),
        P("pipe"),
        P("pipe", None),
        P("pipe"),
    )
    return jax.shard_map(
        local,
        mesh=mesh,
        in_specs=placed,
        out_specs=(
            P("dp", None, "pipe"),
            P("dp", None, "pipe"),
            P("pipe", None),
            P("pipe", None),
            P("pipe", None),
            P("pipe"),
            P("pipe", None),
            P("pipe"),
            P("pipe", "dp"),
            P("pipe"),
            P("pipe", "dp"),
            P("pipe"),
        ),
        check_vma=False,
    )
```

profile of v0, /device:TPU:0, one launch (start us, length us, event | category | flops | bytes accessed | tf_op | source)
XLA Modules:
  0.0 885.4 jit_solution(11936852131019654546)
XLA Ops:
  26.1 7.8 maximum_select_fusion
  40.1 22.9 %conditional.10 = (f32[4,768,384]{2,1,0:T(8,128)}, f32[4,196,3072]{2,1,0:T(8,128)}, bf16[4,196,768]{2,0,1:T(4,128)(2,1)}) conditional(s32[]{:T(128)} %clamp.30, () %tuple.178, (f32[4,196,768]{2,0,1:T(4,128)S(1)}, f32[768]{0:T(1024)S(1)}, f32[768]{0:T(1024)S(1)}, bf16[196,384]{1,0:T(8,128)(2,1)S(1)}, bf16[384]{0:T(512)(128)(2,1)S(1)}, ...), branch_computations={%region_0.1_spmd, %region_1.4_spmd, %region_4.7_spmd} | conditional | flops 7430668800 | bytes 60904736 | solution.py:236
  69.1 9.2 %broadcast_in_dim.367 = f32[2,4,196,3072]{3,2,1,0:T(8,128)} broadcast(f32[]{:T(128)} %constant.807.clone.1), dimensions={} | broadcast | bytes 19267588 | tf_op jit(solution)/shard_map/broadcast_in_dim | solution.py:226
  78.3 9.3 %bitcast_dynamic-update-slice_fusion.4 = f32[2,4,196,3072]{3,2,1,0:T(8,128)} fusion(f32[2,4,196,3072]{3,2,1,0:T(8,128)} %broadcast_in_dim.367, s32[]{:T(128)S(6)} %min.31, f32[4,196,3072]{2,1,0:T(8,128)} %get-tuple-element.1342, pred[]{:T(512)S(6)} %and.41), kind=kLoop, calls=%fused_computation.761 | loop fusion | flops 2408448 | bytes 19660804 | tf_op jit(solution)/shard_map/jit(dynamic_update_index_in_dim)/dynamic_update_slice | solution.py:126
  97.2 8.9 %constant_dynamic-slice_fusion.11 = f32[1,4,196,3072]{3,2,1,0:T(8,128)} fusion(f32[2,4,196,3072]{3,2,1,0:T(8,128)} %bitcast_dynamic-update-slice_fusion.4, s32[]{:T(128)S(6)} %min.32), kind=kLoop, calls=%fused_computation.855 | loop fusion | bytes 19267588 | tf_op jit(solution)/shard_map/jit(dynamic_index_in_dim)/dynamic_slice | solution.py:124
  108.4 22.7 %conditional.11 = (f32[4,768,384]{2,1,0:T(8,128)}, f32[4,196,3072]{2,1,0:T(8,128)}, bf16[4,196,768]{2,0,1:T(4,128)(2,1)}) conditional(s32[]{:T(128)} %clamp.31, () %tuple.181, (f32[4,196,768]{2,0,1:T(4,128)S(1)}, f32[768]{0:T(1024)S(1)}, f32[768]{0:T(1024)S(1)}, bf16[196,384]{1,0:T(8,128)(2,1)S(1)}, bf16[384]{0:T(512)(128)(2,1)S(1)}, ...), branch_computations={%region_7.8_spmd, %region_8.11_spmd, %region_11.14_spmd} | conditional | flops 7430668800 | bytes 60904736 | solution.py:236
  143.5 13.3 %bitcast_dynamic-update-slice_fusion.3 = f32[2,4,196,3072]{3,2,1,0:T(8,128)} fusion(f32[2,4,196,3072]{3,2,1,0:T(8,128)} %bitcast_dynamic-update-slice_fusion.4, s32[]{:T(128)S(6)} %min.32, f32[4,196,3072]{2,1,0:T(8,128)} %get-tuple-element.1343, f32[1,4,196,3072]{3,2,1,0:T(8,128)} %constant_dynamic-slice_fusion.11, pred[]{:T(512)S(6)} %and.44), kind=kLoop, calls=%fused_computation.759 | loop fusion | flops 2408448 | bytes 29491204 | tf_op jit(solution)/shard_map/jit(dynamic_update_index_in_dim)/dynamic_update_slice | solution.py:126
  168.1 8.9 %constant_dynamic-slice_fusion.10 = f32[1,4,196,3072]{3,2,1,0:T(8,128)} fusion(f32[2,4,196,3072]{3,2,1,0:T(8,128)} %bitcast_dynamic-update-slice_fusion.3, s32[]{:T(128)S(6)} %min.33), kind=kLoop, calls=%fused_computation.854 | loop fusion | bytes 19267588 | tf_op jit(solution)/shard_map/jit(dynamic_index_in_dim)/dynamic_slice | solution.py:124
  179.3 14.7 %conditional.12 = (f32[4,768,384]{2,1,0:T(8,128)}, f32[4,196,3072]{2,1,0:T(8,128)}, bf16[4,196,768]{2,0,1:T(4,128)(2,1)}) conditional(s32[]{:T(128)} %clamp.32, () %tuple.184, (f32[4,196,768]{2,0,1:T(4,128)S(1)}, f32[768]{0:T(1024)S(1)}, f32[768]{0:T(1024)S(1)}, bf16[196,384]{1,0:T(8,128)(2,1)S(1)}, ...), branch_computations={%region_14.15_spmd, %region_15.18_spmd, %region_18.21_spmd} | conditional | flops 7430668800 | bytes 60904736 | solution.py:236
  194.1 12.6 %collective-permute-start.10 = (bf16[4,196,768]{2,0,1:T(4,128)(2,1)}, bf16[4,196,768]{2,0,1:T(4,128)(2,1)}, u32[]{:S(2)}, u32[]{:S(2)}) collective-permute-start(bf16[4,196,768]{2,0,1:T(4,128)(2,1)} %get-tuple-element.1654), channel_id=1, source_target_pairs={{0,1},{1,2},{2,3},{4,5},{5,6},{6,7},{8,9},{9,10},{10,11},{12,13},{... | collective-permute-start | bytes 3612680 | tf_op jit(solution)/shard_map/ppermute | solution.py:25
  215.2 10.6 %bitcast_dynamic-update-slice_fusion.2 = f32[2,4,196,3072]{3,2,1,0:T(8,128)} fusion(f32[2,4,196,3072]{3,2,1,0:T(8,128)} %bitcast_dynamic-update-slice_fusion.3, s32[]{:T(128)S(6)} %min.33, f32[4,196,3072]{2,1,0:T(8,128)} %get-tuple-element.1344, f32[1,4,196,3072]{3,2,1,0:T(8,128)} %constant_dynamic-slice_fusion.10, pred[]{:T(512)S(6)} %and.45), kind=kLoop, calls=%fused_computation.757 | loop fusion | flops 2408448 | bytes 29491204 | tf_op jit(solution)/shard_map/jit(dynamic_update_index_in_dim)/dynamic_update_slice | solution.py:126
  235.6 8.9 %constant_dynamic-slice_fusion.9 = f32[1,4,196,3072]{3,2,1,0:T(8,128)} fusion(f32[2,4,196,3072]{3,2,1,0:T(8,128)} %bitcast_dynamic-update-slice_fusion.2, s32[]{:T(128)S(6)} %min.34), kind=kLoop, calls=%fused_computation.853 | loop fusion | bytes 19267588 | tf_op jit(solution)/shard_map/jit(dynamic_index_in_dim)/dynamic_slice | solution.py:124
  246.8 14.8 %conditional.13 = (f32[4,768,384]{2,1,0:T(8,128)}, f32[4,196,3072]{2,1,0:T(8,128)}, bf16[4,196,768]{2,0,1:T(4,128)(2,1)}) conditional(s32[]{:T(128)} %clamp.33, () %tuple.187, (f32[4,196,768]{2,0,1:T(4,128)S(1)}, f32[768]{0:T(1024)S(1)}, f32[768]{0:T(1024)S(1)}, bf16[196,384]{1,0:T(8,128)(2,1)S(1)}, ...), branch_computations={%region_21.22_spmd, %region_22.25_spmd, %region_25.28_spmd} | conditional | flops 7430668800 | bytes 60904736 | solution.py:236
  261.6 8.9 collective-permute-start.11
  279.0 10.6 %bitcast_dynamic-update-slice_fusion.1 = f32[2,4,196,3072]{3,2,1,0:T(8,128)} fusion(f32[2,4,196,3072]{3,2,1,0:T(8,128)} %bitcast_dynamic-update-slice_fusion.2, s32[]{:T(128)S(6)} %min.34, f32[4,196,3072]{2,1,0:T(8,128)} %get-tuple-element.1345, f32[1,4,196,3072]{3,2,1,0:T(8,128)} %constant_dynamic-slice_fusion.9, pred[]{:T(512)S(6)} %and.46), kind=kLoop, calls=%fused_computation.755 | loop fusion | flops 2408448 | bytes 29491204 | tf_op jit(solution)/shard_map/jit(dynamic_update_index_in_dim)/dynamic_update_slice | solution.py:126
  299.3 8.9 %constant_dynamic-slice_fusion.8 = f32[1,4,196,3072]{3,2,1,0:T(8,128)} fusion(f32[2,4,196,3072]{3,2,1,0:T(8,128)} %bitcast_dynamic-update-slice_fusion.1, s32[]{:T(128)S(6)} %min.35), kind=kLoop, calls=%fused_computation.852 | loop fusion | bytes 19267588 | tf_op jit(solution)/shard_map/jit(dynamic_index_in_dim)/dynamic_slice | solution.py:124
  310.6 14.2 %conditional.14 = (f32[4,768,384]{2,1,0:T(8,128)}, f32[4,196,3072]{2,1,0:T(8,128)}, bf16[4,196,768]{2,0,1:T(4,128)(2,1)}) conditional(s32[]{:T(128)} %clamp.34, () %tuple.190, (f32[4,196,768]{2,0,1:T(4,128)S(1)}, f32[768]{0:T(1024)S(1)}, f32[768]{0:T(1024)S(1)}, bf16[196,384]{1,0:T(8,128)(2,1)S(1)}, ...), branch_computations={%region_28.29_spmd, %region_29.32_spmd, %region_32.35_spmd} | conditional | flops 7430668800 | bytes 60904736 | solution.py:236
  333.9 10.6 %bitcast_dynamic-update-slice_fusion = f32[2,4,196,3072]{3,2,1,0:T(8,128)} fusion(f32[2,4,196,3072]{3,2,1,0:T(8,128)} %bitcast_dynamic-update-slice_fusion.1, s32[]{:T(128)S(6)} %min.35, f32[4,196,3072]{2,1,0:T(8,128)} %get-tuple-element.1346, f32[1,4,196,3072]{3,2,1,0:T(8,128)} %constant_dynamic-slice_fusion.8, pred[]{:T(512)S(6)} %and.47), kind=kLoop, calls=%fused_computation.753 | loop fusion | flops 2408448 | bytes 29491204 | tf_op jit(solution)/shard_map/jit(dynamic_update_index_in_dim)/dynamic_update_slice | solution.py:126
  349.6 17.9 %conditional.15 = (f32[768]{0:T(1024)S(1)}, f32[768]{0:T(1024)S(1)}, f32[196,384]{1,0:T(8,128)S(1)}, f32[384]{0:T(512)S(1)}, f32[384,196]{0,1:T(8,128)S(1)}, /*i...) conditional(s32[]{:T(128)} %clamp.35, () %tuple.193, ...), branch_computations={%region_36.37_spmd, %region_37.46_spmd, %region_46.55_spmd} | conditional | flops 14893841408 | bytes 201422880 | solution.py:301
  375.8 9.5 %conditional.16 = (f32[768]{0:T(1024)S(1)}, f32[768]{0:T(1024)S(1)}, f32[196,384]{1,0:T(8,128)S(1)}, f32[384]{0:T(512)S(1)}, f32[384,196]{0,1:T(8,128)S(1)}, /*i...) conditional(s32[]{:T(128)} %clamp.36, (f32[768]{0:T(1024)S(1)}, ...), branch_computations={%region_55.56_spmd, %region_56.65_spmd, %region_65.74_spmd} | conditional | flops 14898566144 | bytes 193239744 | solution.py:301
  397.9 7.7 collective-permute-done.13
  408.6 9.3 %conditional.17 = (f32[768]{0:T(1024)S(1)}, f32[768]{0:T(1024)S(1)}, f32[196,384]{1,0:T(8,128)S(1)}, f32[384]{0:T(512)S(1)}, f32[384,196]{0,1:T(8,128)S(1)}, /*i...) conditional(s32[]{:T(128)} %clamp.37, (f32[768]{0:T(1024)S(1)}, ...), branch_computations={%region_74.75_spmd, %region_75.84_spmd, %region_84.93_spmd} | conditional | flops 14898566144 | bytes 193239744 | solution.py:301
  424.0 93.4 %collective-permute-done.14 = bf16[4,196,768]{2,0,1:T(4,128)(2,1)} collective-permute-done((bf16[4,196,768]{2,0,1:T(4,128)(2,1)}, bf16[4,196,768]{2,0,1:T(4,128)(2,1)}, u32[]{:S(2)}, u32[]{:S(2)}) %collective-permute-start.14) | collective-permute-done | bytes 1204256 | tf_op jit(solution)/shard_map/ppermute | solution.py:25
  519.7 31.5 %conditional.18 = (f32[768]{0:T(1024)S(1)}, f32[768]{0:T(1024)S(1)}, f32[196,384]{1,0:T(8,128)S(1)}, f32[384]{0:T(512)S(1)}, f32[384,196]{0,1:T(8,128)S(1)}, /*i...) conditional(s32[]{:T(128)} %clamp.38, (f32[768]{0:T(1024)S(1)}, ...), branch_computations={%region_93.94_spmd, %region_94.103_spmd, %region_103.112_spmd} | conditional | flops 14898566144 | bytes 193239744 | solution.py:301
  561.5 31.9 %collective-permute-done.15 = bf16[4,196,768]{2,0,1:T(4,128)(2,1)S(1)} collective-permute-done((bf16[4,196,768]{2,0,1:T(4,128)(2,1)S(1)}, bf16[4,196,768]{2,0,1:T(4,128)(2,1)S(1)}, u32[]{:S(2)}, u32[]{:S(2)}) %collective-permute-start.15) | collective-permute-done | bytes 1204256 | tf_op jit(solution)/shard_map/ppermute | solution.py:25
  594.4 28.0 %conditional.19 = (f32[768]{0:T(1024)S(1)}, f32[768]{0:T(1024)S(1)}, f32[196,384]{1,0:T(8,128)S(1)}, f32[384]{0:T(512)S(1)}, f32[384,196]{0,1:T(8,128)S(1)}, /*i...) conditional(s32[]{:T(128)} %clamp.39, (f32[768]{0:T(1024)S(1)}, ...), branch_computations={%region_112.113_spmd, %region_113.122_spmd, %region_122.131_spmd} | conditional | flops 14898566144 | bytes 193239744 | solution.py:301
  632.5 9.9 %copy.105 = f32[3072,768]{0,1:T(8,128)} copy(f32[3072,768]{1,0:T(8,128)} %get-tuple-element.1400) | data formatting | bytes 18874368 | tf_op jit(solution)/shard_map/cond | solution.py:301
  651.3 7.4 convert_add_fusion
  667.6 7.5 convert_add_fusion.1
  677.4 39.6 %all-reduce = (f32[1,768]{1,0:T(1,128)}, f32[1,768]{1,0:T(1,128)}, f32[192]{0:T(256)}, f32[98]{0:T(128)}, f32[1536]{0:T(1024)}, /*index=5*/f32[384]{0:T(512)}) all-reduce(f32[1,768]{1,0:T(1,128)S(1)} %broadcast_in_dim.378, f32[1,768]{1,0:T(1,128)S(1)} %broadcast_in_dim.379, ...), channel_id=1, replica_groups=mesh['dp'=8,'pipe'=4] {'dp'}, use_global_device_ids=true, to_apply=%region_132.133 | all-reduce | flops 3746 | bytes 29968 | tf_op jit(solution)/shard_map/psum | solution.py:355
  717.0 58.3 %reduce-scatter.11.cloned.1.call-done = f32[1536,96]{0,1:T(8,128)} async-done(((f32[1536,768]{0,1:T(8,128)}), f32[1536,96]{0,1:T(8,128)}) %reduce-scatter.11.cloned.1.call-update) | async-done | bytes 589840 | tf_op jit(solution)/shard_map/reduce_scatter | solution.py:353
  775.3 99.5 %reduce-scatter.9.cloned.1.call-done = f32[384,384]{1,0:T(8,128)} async-done(((f32[384,3072]{1,0:T(8,128)}), f32[384,384]{1,0:T(8,128)}) %reduce-scatter.9.cloned.1.call-update) | async-done | bytes 589840 | tf_op jit(solution)/shard_map/reduce_scatter | solution.py:352
  (354 shorter events, 316.6 us)
Async XLA Ops:
  8.0 709.0 %reduce-scatter.5.cloned.1.call-start = ((), (), s32[]{:S(2)}) async-start(), calls=%async_computation.4 | async-start | bytes 3932160 | tf_op jit(solution)/shard_map/reduce_scatter | solution.py:321
  8.1 18.0 %collective-permute-start.4 = (bf16[384,3072]{1,0:T(8,128)(2,1)}, bf16[384,3072]{1,0:T(8,128)(2,1)}, u32[]{:S(2)}, u32[]{:S(2)}) collective-permute-start(bf16[384,3072]{1,0:T(8,128)(2,1)} %param.54), channel_id=1, source_target_pairs={{0,1},{1,0},{2,3},{3,2},{4,5},{5,4},{6,7},{7,6},{8,9},{9,8},{10,11... | collective-permute-start | bytes 7077896 | tf_op jit(solution)/shard_map/ppermute | solution.py:19
  8.6 25.3 %collective-permute-start.6 = (bf16[1536,768]{1,0:T(8,128)(2,1)}, bf16[1536,768]{1,0:T(8,128)(2,1)}, u32[]{:S(2)}, u32[]{:S(2)}) collective-permute-start(bf16[1536,768]{1,0:T(8,128)(2,1)} %param.56), channel_id=1, source_target_pairs={{0,1},{1,0},{2,3},{3,2},{4,5},{5,4},{6,7},{7,6},{8,9},{9,8},{10,11... | collective-permute-start | bytes 7077896 | tf_op jit(solution)/shard_map/ppermute | solution.py:19
  8.7 16.4 %collective-permute-start.5 = (bf16[1536]{0:T(1024)(128)(2,1)}, bf16[1536]{0:T(1024)(128)(2,1)S(1)}, u32[]{:S(2)}, u32[]{:S(2)}) collective-permute-start(bf16[1536]{0:T(1024)(128)(2,1)} %param.55), channel_id=1, source_target_pairs={{0,1},{1,0},{2,3},{3,2},{4,5},{5,4},{6,7},{7,6},{8,9},{9,8},{10,11... | collective-permute-start | bytes 9224 | tf_op jit(solution)/shard_map/ppermute | solution.py:19
  9.1 15.6 %collective-permute-start.7 = (bf16[384]{0:T(512)(128)(2,1)}, bf16[384]{0:T(512)(128)(2,1)S(1)}, u32[]{:S(2)}, u32[]{:S(2)}) collective-permute-start(bf16[384]{0:T(512)(128)(2,1)} %param.57), channel_id=1, source_target_pairs={{0,1},{1,0},{2,3},{3,2},{4,5},{5,4},{6,7},{7,6},{8,9},{9,8},{10,11... | collective-permute-start | bytes 2312 | tf_op jit(solution)/shard_map/ppermute | solution.py:19
  9.2 14.1 %collective-permute-start.3 = (bf16[98]{0:T(256)(128)(2,1)}, bf16[98]{0:T(256)(128)(2,1)S(1)}, u32[]{:S(2)}, u32[]{:S(2)}) collective-permute-start(bf16[98]{0:T(256)(128)(2,1)} %param.53), channel_id=1, source_target_pairs={{0,1},{1,0},{2,3},{3,2},{4,5},{5,4},{6,7},{7,6},{8,9},{9,8},{10,11... | collective-permute-start | bytes 596 | tf_op jit(solution)/shard_map/ppermute | solution.py:19
  23.2 1.1 collective-permute-start.1
  24.4 1.3 collective-permute-start.2
  24.6 1.3 collective-permute-start
  63.0 43.1 %collective-permute-start.8 = (bf16[4,196,768]{2,0,1:T(4,128)(2,1)}, bf16[4,196,768]{2,0,1:T(4,128)(2,1)S(1)}, u32[]{:S(2)}, u32[]{:S(2)}) collective-permute-start(bf16[4,196,768]{2,0,1:T(4,128)(2,1)} %get-tuple-element.1652), channel_id=1, source_target_pairs={{0,1},{1,2},{2,3},{4,5},{5,6},{6,7},{8,9},{9,10},{10,11},{12,13},{... | collective-permute-start | bytes 3612680 | tf_op jit(solution)/shard_map/ppermute | solution.py:25
  131.2 45.8 %collective-permute-start.9 = (bf16[4,196,768]{2,0,1:T(4,128)(2,1)}, bf16[4,196,768]{2,0,1:T(4,128)(2,1)}, u32[]{:S(2)}, u32[]{:S(2)}) collective-permute-start(bf16[4,196,768]{2,0,1:T(4,128)(2,1)} %get-tuple-element.1653), channel_id=1, source_target_pairs={{0,1},{1,2},{2,3},{4,5},{5,6},{6,7},{8,9},{9,10},{10,11},{12,13},{... | collective-permute-start | bytes 3612680 | tf_op jit(solution)/shard_map/ppermute | solution.py:25
  194.1 50.4 %collective-permute-start.10 = (bf16[4,196,768]{2,0,1:T(4,128)(2,1)}, bf16[4,196,768]{2,0,1:T(4,128)(2,1)}, u32[]{:S(2)}, u32[]{:S(2)}) collective-permute-start(bf16[4,196,768]{2,0,1:T(4,128)(2,1)} %get-tuple-element.1654), channel_id=1, source_target_pairs={{0,1},{1,2},{2,3},{4,5},{5,6},{6,7},{8,9},{9,10},{10,11},{12,13},{... | collective-permute-start | bytes 3612680 | tf_op jit(solution)/shard_map/ppermute | solution.py:25
  261.6 46.6 %collective-permute-start.11 = (bf16[4,196,768]{2,0,1:T(4,128)(2,1)}, bf16[4,196,768]{2,0,1:T(4,128)(2,1)}, u32[]{:S(2)}, u32[]{:S(2)}) collective-permute-start(bf16[4,196,768]{2,0,1:T(4,128)(2,1)} %get-tuple-element.1655), channel_id=1, source_target_pairs={{0,1},{1,2},{2,3},{4,5},{5,6},{6,7},{8,9},{9,10},{10,11},{12,13},{... | collective-permute-start | bytes 3612680 | tf_op jit(solution)/shard_map/ppermute | solution.py:25
  367.5 5.3 collective-permute-start.12
  388.1 17.4 %collective-permute-start.13 = (bf16[4,196,768]{2,0,1:T(4,128)(2,1)}, bf16[4,196,768]{2,0,1:T(4,128)(2,1)}, u32[]{:S(2)}, u32[]{:S(2)}) collective-permute-start(bf16[4,196,768]{2,0,1:T(4,128)(2,1)} %copy.93), channel_id=1, source_target_pairs={{1,0},{2,1},{3,2},{5,4},{6,5},{7,6},{9,8},{10,9},{11,10},{13,12},{... | collective-permute-start | bytes 3612680 | tf_op jit(solution)/shard_map/ppermute | solution.py:25
  397.8 319.2 %all-reduce.4.cloned.1.call-start = ((), (), s32[]{:S(2)}) async-start(), calls=%async_computation.8 | async-start | bytes 712704 | tf_op jit(solution)/shard_map/psum | solution.py:355
  420.7 96.7 %collective-permute-start.14 = (bf16[4,196,768]{2,0,1:T(4,128)(2,1)}, bf16[4,196,768]{2,0,1:T(4,128)(2,1)}, u32[]{:S(2)}, u32[]{:S(2)}) collective-permute-start(bf16[4,196,768]{2,0,1:T(4,128)(2,1)} %copy.96), channel_id=1, source_target_pairs={{1,0},{2,1},{3,2},{5,4},{6,5},{7,6},{9,8},{10,9},{11,10},{13,12},{... | collective-permute-start | bytes 3612680 | tf_op jit(solution)/shard_map/ppermute | solution.py:25
  422.7 94.7 %copy-start.48 = (bf16[8,196,768]{2,0,1:T(8,128)(2,1)S(1)}, bf16[8,196,768]{2,0,1:T(8,128)(2,1)}, u32[]{:S(2)}) copy-start(bf16[8,196,768]{2,0,1:T(8,128)(2,1)} %param.45) | copy-start | bytes 7225348
  424.0 95.6 %copy-start.1 = (f32[4,196,768]{2,1,0:T(8,128)S(1)}, f32[4,196,768]{2,1,0:T(8,128)}, u32[]{:S(2)}) copy-start(f32[4,196,768]{2,1,0:T(8,128)} %get-tuple-element.1790) | copy-start | bytes 7225348
  424.0 95.6 %copy-start.83 = (f32[4]{0:T(128)S(1)}, f32[4]{0:T(128)}, u32[]{:S(2)}) copy-start(f32[4]{0:T(128)} %get-tuple-element.1802) | copy-start | bytes 52
  553.1 40.3 %collective-permute-start.15 = (bf16[4,196,768]{2,0,1:T(4,128)(2,1)S(1)}, bf16[4,196,768]{2,0,1:T(4,128)(2,1)S(1)}, u32[]{:S(2)}, u32[]{:S(2)}) collective-permute-start(bf16[4,196,768]{2,0,1:T(4,128)(2,1)S(1)} %copy.99), channel_id=1, source_target_pairs={{1,0},{2,1},{3,2},{5,4},{6,5},{7,6},{9,8},{10,9},{11,10},{13,12},{... | collective-permute-start | bytes 3612680 | tf_op jit(solution)/shard_map/ppermute | solution.py:25
  622.6 4.4 collective-permute-start.18
  622.7 3.5 collective-permute-start.16
  627.7 89.3 %reduce-scatter.7.cloned.1.call-start = ((), (), s32[]{:S(2)}) async-start(), calls=%async_computation.5 | async-start | bytes 3932160 | tf_op jit(solution)/shard_map/reduce_scatter | solution.py:322
  632.4 142.9 %reduce-scatter.11.cloned.1.call-start = ((), (), s32[]{:S(2)}) async-start(), calls=%async_computation.7 | async-start | bytes 5308416 | tf_op jit(solution)/shard_map/reduce_scatter | solution.py:353
  646.7 4.6 collective-permute-start.22
  658.7 216.1 %reduce-scatter.9.cloned.1.call-start = ((), (), s32[]{:S(2)}) async-start(), calls=%async_computation.6 | async-start | bytes 5308416 | tf_op jit(solution)/shard_map/reduce_scatter | solution.py:352
  663.0 4.6 collective-permute-start.20
  675.2 2.2 collective-permute-start.23
  675.5 1.9 collective-permute-start.21
  675.8 1.1 collective-permute-start.19
  676.1 1.1 collective-permute-start.17
  (60 other events, 666.4 us)
Sparse Core Ops, SparseCore 0:
  397.9 111.4 reduce-scatter.4
  632.6 38.5 reduce-scatter.6
  675.8 99.4 reduce-scatter.10
  779.8 94.9 reduce-scatter.8
Sparse Core Ops, SparseCore 1:
  627.8 82.5 all-reduce.3
where the time goes:
time: 892 us; the launch traced here: 885 us
  waiting for transfers between devices  306 us (34%)
  local copies, waits for them, and re-layouts  188 us (21%)
  other arithmetic  184 us (21%)
  loops' own time  68.8 us (8%)
  matrix products  47.8 us (5%)
  blocking collectives  39.6 us (4%)
  starting transfers between devices  35 us (4%)
  between operations  16.3 us (2%)
    ppermute x8, waiting for transfers between devices, from_behind(): return lax.ppermute(x, axis, pairs)  137 us
    reduce_scatter x1, waiting for transfers between devices, local(): lax.psum_scatter(joined[4], 'dp', scatter_dimension=1, tiled=True)  99.5 us
    dynamic_update_slice x14, other arithmetic, store_slot(): return lax.dynamic_update_index_in_dim(buffer, chosen, slot_index, 0)  85.6 us
    dynamic_slice x20, local copies, waits for them, and re-layouts, store_slot(): current = lax.dynamic_index_in_dim(buffer, slot_index, 0, keepdims=False)  69.5 us
    reduce_scatter x1, waiting for transfers between devices, local(): lax.psum_scatter(joined[6], 'dp', scatter_dimension=1, tiled=True)  58.3 us
    another operation x20, local copies, waits for them, and re-layouts  40.3 us
    psum x1, blocking collectives, local(): lax.psum((grad_totals[0], grad_totals[1], joined[0], joined[1], joined[2]...  39.6 us
    another operation x5, loops' own time, local(): lax.switch(branch_pick, [spare_backward, token_backward, chan_backward],...  37.7 us
  transfers between devices with their start and end apart: 29, of which 13 were waited for; matrix products, arithmetic and copies ran while one was open for 32% of the time, Pallas kernels for 0%

commit v1 on v0

v1 whole, which is shorter than its diff:
```python
import functools

import jax
import jax.numpy as jnp
from jax import lax
from jax.experimental import pallas as pl
from jax.experimental.pallas import tpu as pltpu
from jax.sharding import PartitionSpec as P

F32 = jnp.float32
BF16 = jnp.bfloat16
NORM_EPS = 1e-06
GELU_SCALE = 0.7978845608
GELU_CUBE = 0.044715
STEPS = 6
SLOTS = 4
VMEM_BYTES = 26 << 20

IN_VMEM = pl.BlockSpec(memory_space=pltpu.VMEM)
IN_ANY = pl.BlockSpec(memory_space=pl.ANY)
IN_SMEM = pl.BlockSpec(memory_space=pltpu.SMEM)

ON, VALID, CROSSING, IMAGE, OTHER = range(5)


def flipped(block, axis, distance):
    count = lax.axis_size(axis)
    route = [(i, i ^ distance) for i in range(count) if i ^ distance < count]
    return lax.ppermute(block, axis, route)


def mm(left, right):
    return lax.dot_general(left, right, (((1,), (0,)), ((), ())), preferred_element_type=F32)


def mm_nt(left, right):
    return lax.dot_general(left, right, (((1,), (1,)), ((), ())), preferred_element_type=F32)


def mm_tn(left, right):
    return lax.dot_general(left, right, (((0,), (0,)), ((), ())), preferred_element_type=F32)


def gelu_pair(pre):
    square = pre * pre
    gate = 0.5 + 0.5 * jnp.tanh(pre * (GELU_SCALE + (GELU_SCALE * GELU_CUBE) * square))
    value = pre * gate
    slope = gate + value * (1.0 - gate) * (2 * GELU_SCALE + (6 * GELU_SCALE * GELU_CUBE) * square)
    return value, slope


def normalised(hidden):
    centred = hidden - jnp.mean(hidden, axis=-1, keepdims=True)
    scale = lax.rsqrt(jnp.mean(centred * centred, axis=-1, keepdims=True) + NORM_EPS)
    return centred * scale, scale


def forward_body(near_slot, far_slot, tab, images, recv, up, down, up_t, down_t, up_col, down_col, u_row, w_row, gains, shifts,
                 send_o, res_o, z_o, gz_o, zt_o, gt_o, h0_o, h1_o, n2_o,
                 x_v, z_v, gz_v, zt_v, gt_v, h1_v, n2_v, h2_v, x_sem, s_sem, o_sems):
    far = tab[5, 0] == 1
    job = jnp.where(far, far_slot, near_slot)
    slot = jnp.maximum(job, 0)
    has_job = job >= 0
    on = has_job & (tab[ON, slot] == 1)
    from_recv = far & (tab[CROSSING, slot] == 1)

    @pl.when(has_job & from_recv)
    def _():
        pltpu.make_async_copy(recv, x_v, x_sem).start()

    @pl.when(has_job & jnp.logical_not(from_recv))
    def _():
        pltpu.make_async_copy(images.at[tab[IMAGE, slot]], x_v, x_sem).start()

    @pl.when(has_job)
    def _():
        pltpu.make_async_copy(recv, x_v, x_sem).wait()

    def deliver():
        copy = pltpu.make_async_copy(h2_v, res_o.at[slot], x_sem)
        copy.start()

        @pl.when(jnp.logical_not(far))
        def _():
            sent = pltpu.make_async_copy(h2_v, send_o, s_sem)
            sent.start()
            sent.wait()

        copy.wait()

    @pl.when(has_job & jnp.logical_not(on))
    def _():
        h2_v[...] = x_v[...] * tab[VALID, slot].astype(F32).astype(BF16)
        deliver()

    @pl.when(on)
    def _():
        started = []

        def put(source, target):
            copy = pltpu.make_async_copy(source, target.at[slot], o_sems.at[len(started)])
            copy.start()
            started.append(copy)

        put(x_v, h0_o)
        h0 = x_v[...].astype(F32)
        centred, _ = normalised(h0)
        n1 = (centred * gains[0:1, :] + shifts[0:1, :]).astype(BF16)
        value, slope = gelu_pair(mm(up_t[...], n1) + up_col[...])
        value = value.astype(BF16)
        zt_v[...] = value
        gt_v[...] = slope.astype(BF16)
        put(zt_v, zt_o)
        put(gt_v, gt_o)
        h1 = (h0 + (mm(down_t[...], value) + down_col[...])).astype(BF16)
        h1_v[...] = h1
        put(h1_v, h1_o)
        h1 = h1.astype(F32)
        centred, _ = normalised(h1)
        n2_v[...] = (centred * gains[1:2, :] + shifts[1:2, :]).astype(BF16)
        put(n2_v, n2_o)
        total = h1 + w_row[...]
        width = up.shape[1] // STEPS
        for step in range(STEPS):
            cols = slice(step * width, (step + 1) * width)
            value, slope = gelu_pair(mm(n2_v[...], up[:, cols]) + u_row[:, cols])
            value = value.astype(BF16)
            z_v[:, cols] = value
            gz_v[:, cols] = slope.astype(BF16)
            total = total + mm(value, down[cols, :])
        put(z_v, z_o)
        put(gz_v, gz_o)
        h2_v[...] = total.astype(BF16)
        deliver()
        for copy in started:
            copy.wait()


def backward_body(near_slot, far_slot, tab, cots, recv, up, down, up_w, down_w, gains, shifts, gz_i, zt_i, gt_i, h0_i, h1_i,
                  send_o, res_o, f_o, dq_o, da_o, db_o, vec_o,
                  e_v, gz_v, zt_v, gt_v, h0_v, h1_v, f_v, dq_v, da_v, db_v, vec_v, e_sem, s_sem, i_sems, o_sems):
    far = tab[5, 0] == 1
    job = jnp.where(far, far_slot, tab[5, 3] if near_slot is None else near_slot)
    slot = jnp.maximum(job, 0)
    has_job = job >= 0
    on = has_job & (tab[ON, slot] == 1)
    from_recv = jnp.logical_not(far) & (tab[CROSSING, slot] == 1)
    channels = up.shape[0]
    rows = e_v.shape[0]
    hidden_t = zt_v.shape[0]
    saved = ((gz_i, gz_v), (h1_i, h1_v), (gt_i, gt_v), (h0_i, h0_v), (zt_i, zt_v))

    def load(i):
        return pltpu.make_async_copy(saved[i][0].at[slot], saved[i][1], i_sems.at[i])

    @pl.when(has_job & from_recv)
    def _():
        pltpu.make_async_copy(recv, e_v, e_sem).start()

    @pl.when(has_job & jnp.logical_not(from_recv))
    def _():
        pltpu.make_async_copy(cots.at[tab[IMAGE, slot]], e_v, e_sem).start()

    @pl.when(on)
    def _():
        for i in range(5):
            load(i).start()

    @pl.when(has_job)
    def _():
        pltpu.make_async_copy(recv, e_v, e_sem).wait()

    def deliver(source):
        copy = pltpu.make_async_copy(source, res_o.at[slot], e_sem)
        copy.start()

        @pl.when(far)
        def _():
            sent = pltpu.make_async_copy(source, send_o, s_sem)
            sent.start()
            sent.wait()

        copy.wait()

    @pl.when(has_job & jnp.logical_not(on))
    def _():
        f_v[...] = e_v[...] * tab[VALID, slot].astype(F32).astype(BF16)
        deliver(f_v)

    @pl.when(on)
    def _():
        started = []

        def put(source, target):
            copy = pltpu.make_async_copy(source, target.at[slot], o_sems.at[len(started)])
            copy.start()
            started.append(copy)

        put(e_v, f_o)
        grad = e_v[...].astype(F32)
        vec_v[...] = jnp.zeros_like(vec_v)
        vec_v[1:2, 0:channels] = jnp.sum(grad, axis=0, keepdims=True)
        dn = jnp.zeros((rows, channels), F32)
        width = up.shape[1] // STEPS
        load(0).wait()
        for step in range(STEPS):
            cols = slice(step * width, (step + 1) * width)
            dq = (mm_nt(e_v[...], down[cols, :]) * gz_v[:, cols].astype(F32)).astype(BF16)
            dq_v[:, cols] = dq
            vec_v[0:1, cols] = jnp.sum(dq.astype(F32), axis=0, keepdims=True)
            dn = dn + mm_nt(dq, up[:, cols])
        put(dq_v, dq_o)

        def norm_back(hidden, dn, grad, row):
            centred, scale = normalised(hidden)
            vec_v[2 + row:3 + row, 0:channels] = jnp.sum(dn * centred, axis=0, keepdims=True)
            vec_v[4 + row:5 + row, 0:channels] = jnp.sum(dn, axis=0, keepdims=True)
            scaled = dn * gains[row:row + 1, :]
            along = jnp.mean(scaled * centred, axis=-1, keepdims=True)
            flat = jnp.mean(scaled, axis=-1, keepdims=True)
            return centred, grad + scale * (scaled - flat - centred * along)

        load(1).wait()
        _, grad = norm_back(h1_v[...].astype(F32), dn, grad, 1)
        f1 = grad.astype(BF16)
        grad = f1.astype(F32)
        load(2).wait()
        dq = (mm(down_w[...], f1) * gt_v[...].astype(F32)).astype(BF16)
        load(3).wait()
        centred, grad = norm_back(h0_v[...].astype(F32), mm(up_w[...], dq), grad, 0)
        f_v[...] = grad.astype(BF16)
        n1 = (centred * gains[0:1, :] + shifts[0:1, :]).astype(BF16)
        load(4).wait()
        da_v[...] = mm_nt(n1, dq)
        db_v[...] = mm_nt(zt_v[...], f1)
        ones = jnp.ones((8, channels), BF16)
        vec_v[6:7, 0:hidden_t] = mm_nt(ones, dq)[0:1]
        vec_v[7:8, 0:rows] = mm_nt(ones, f1)[0:1]
        put(da_v, da_o)
        put(db_v, db_o)
        put(vec_v, vec_o)
        deliver(f_v)
        for copy in started:
            copy.wait()


def kept_call(body, ins, specs, kept, shapes, scratch, cost, name):
    aliases = {}
    passed = 0
    for position, array in enumerate(kept):
        if array is not None:
            aliases[len(ins) + passed] = position
            passed += 1
    first = len(ins)

    def trimmed(*refs):
        body(*refs[:first], *refs[first + passed:])

    return pl.pallas_call(
        trimmed,
        out_shape=shapes,
        in_specs=specs + [IN_ANY] * passed,
        out_specs=[IN_ANY] * len(shapes),
        input_output_aliases=aliases,
        scratch_shapes=scratch,
        compiler_params=pltpu.CompilerParams(vmem_limit_bytes=VMEM_BYTES),
        cost_estimate=cost,
        name=name,
    )(*ins, *[array for array in kept if array is not None])


def forward_call(slots, tab, images, recv, w, kept):
    rows, channels = recv.shape
    ff = w["up"].shape[1]
    hidden_t = w["up_t"].shape[0]
    shape = jax.ShapeDtypeStruct
    shapes = [shape((rows, channels), BF16), shape((SLOTS, rows, channels), BF16),
              shape((SLOTS, rows, ff), BF16), shape((SLOTS, rows, ff), BF16),
              shape((SLOTS, hidden_t, channels), BF16), shape((SLOTS, hidden_t, channels), BF16),
              shape((SLOTS, rows, channels), BF16), shape((SLOTS, rows, channels), BF16),
              shape((SLOTS, rows, channels), BF16)]
    ins = [tab, images, recv] + [w[k] for k in ("up", "down", "up_t", "down_t", "up_col", "down_col", "u_row", "w_row", "gains", "shifts")]
    scratch = [pltpu.VMEM((rows, channels), BF16), pltpu.VMEM((rows, ff), BF16), pltpu.VMEM((rows, ff), BF16),
               pltpu.VMEM((hidden_t, channels), BF16), pltpu.VMEM((hidden_t, channels), BF16),
               pltpu.VMEM((rows, channels), BF16), pltpu.VMEM((rows, channels), BF16), pltpu.VMEM((rows, channels), BF16),
               pltpu.SemaphoreType.DMA, pltpu.SemaphoreType.DMA, pltpu.SemaphoreType.DMA((7,))]
    cost = pl.CostEstimate(flops=4 * rows * channels * (ff + hidden_t), bytes_accessed=8 * rows * ff, transcendentals=rows * ff)
    return kept_call(functools.partial(forward_body, *slots), ins, [IN_SMEM, IN_ANY, IN_ANY] + [IN_VMEM] * 10,
                     kept, shapes, scratch, cost, "forward_slot")


def backward_call(slots, tab, cots, recv, w, saved, kept):
    rows, channels = recv.shape
    ff = w["up"].shape[1]
    hidden_t = w["up_t"].shape[0]
    shape = jax.ShapeDtypeStruct
    shapes = [shape((rows, channels), BF16), shape((SLOTS, rows, channels), BF16),
              shape((SLOTS, rows, channels), BF16), shape((SLOTS, rows, ff), BF16),
              shape((SLOTS, rows, hidden_t), F32), shape((SLOTS, hidden_t, rows), F32), shape((SLOTS, 8, ff), F32)]
    ins = [tab, cots, recv] + [w[k] for k in ("up", "down", "up_w", "down_w", "gains", "shifts")] + list(saved)
    scratch = [pltpu.VMEM((rows, channels), BF16), pltpu.VMEM((rows, ff), BF16),
               pltpu.VMEM((hidden_t, channels), BF16), pltpu.VMEM((hidden_t, channels), BF16),
               pltpu.VMEM((rows, channels), BF16), pltpu.VMEM((rows, channels), BF16), pltpu.VMEM((rows, channels), BF16),
               pltpu.VMEM((rows, ff), BF16), pltpu.VMEM((rows, hidden_t), F32), pltpu.VMEM((hidden_t, rows), F32), pltpu.VMEM((8, ff), F32),
               pltpu.SemaphoreType.DMA, pltpu.SemaphoreType.DMA, pltpu.SemaphoreType.DMA((5,)), pltpu.SemaphoreType.DMA((5,))]
    cost = pl.CostEstimate(flops=4 * rows * channels * (ff + 2 * hidden_t), bytes_accessed=8 * rows * ff, transcendentals=0)
    return kept_call(functools.partial(backward_body, *slots), ins, [IN_SMEM, IN_ANY, IN_ANY] + [IN_VMEM] * 6 + [IN_ANY] * 5,
                     kept, shapes, scratch, cost, "backward_slot")


def down_grad_body(chunk, count, aligned, tab, f_i, recv, cots, z_i, out, f_v, z_v, f_sems, z_sems):
    half = tab[5, 1]
    me = tab[5, 2]
    late = tab[5, 3]
    width = out.shape[-1]
    channels = f_i.shape[2]
    rows = f_i.shape[1]
    size = z_i.shape[2] // 2

    def copies(slot, side):
        first = pl.multiple_of(jnp.where(side == 0, 1 - half, half) * size + chunk * width, 128)
        return pltpu.make_async_copy(z_i.at[slot, :, pl.ds(first, width)], z_v.at[side, pl.ds(slot * rows, rows), :], z_sems.at[side, slot])

    def f_copy(slot, source):
        return pltpu.make_async_copy(source, f_v.at[pl.ds(slot * rows, rows), :], f_sems.at[slot])

    for slot in range(SLOTS):
        on = tab[ON, slot] == 1

        crossed = tab[CROSSING, slot] == 1

        @pl.when(on & (late == slot) & crossed)
        def _():
            f_copy(slot, recv).start()

        @pl.when(on & (late == slot) & jnp.logical_not(crossed))
        def _():
            f_copy(slot, cots.at[tab[IMAGE, slot]]).start()

        @pl.when(on & (late != slot))
        def _():
            f_copy(slot, f_i.at[slot]).start()

        @pl.when(on)
        def _():
            for side in range(2):
                copies(slot, side).start()

        @pl.when(jnp.logical_not(on))
        def _():
            f_v[pl.ds(slot * rows, rows), :] = jnp.zeros((rows, channels), BF16)
            for side in range(2):
                z_v[side, pl.ds(slot * rows, rows), :] = jnp.zeros((rows, width), BF16)

    for slot in range(SLOTS):
        @pl.when(tab[ON, slot] == 1)
        def _():
            f_copy(slot, recv).wait()
            for side in range(2):
                copies(slot, side).wait()

    f_t = f_v[...].T
    piece = channels // count
    for side in range(2):
        total = mm(f_t, z_v[side]).astype(BF16)
        if aligned:
            for d in range(count):
                out[side, d ^ me] = total[d * piece:(d + 1) * piece]
        else:
            out[side] = total


def up_grad_body(chunk, count, aligned, tab, n_i, dq_i, out, n_v, dq_v, n_sems, dq_sems):
    half = tab[5, 1]
    me = tab[5, 2]
    height = out.shape[-2]
    rows = n_i.shape[1]
    size = n_i.shape[2] // 2
    ff = dq_i.shape[2]

    def n_copy(slot):
        return pltpu.make_async_copy(n_i.at[slot], n_v.at[pl.ds(slot * rows, rows), :], n_sems.at[slot])

    def dq_copy(slot):
        return pltpu.make_async_copy(dq_i.at[slot], dq_v.at[pl.ds(slot * rows, rows), :], dq_sems.at[slot])

    for slot in range(SLOTS):
        on = tab[ON, slot] == 1

        @pl.when(on)
        def _():
            n_copy(slot).start()
            dq_copy(slot).start()

        @pl.when(jnp.logical_not(on))
        def _():
            n_v[pl.ds(slot * rows, rows), :] = jnp.zeros((rows, 2 * size), BF16)
            dq_v[pl.ds(slot * rows, rows), :] = jnp.zeros((rows, ff), BF16)

    for slot in range(SLOTS):
        @pl.when(tab[ON, slot] == 1)
        def _():
            n_copy(slot).wait()
            dq_copy(slot).wait()

    piece = ff // count
    for fixed in range(2):
        first = fixed * size + chunk * height
        n_t = n_v[:, first - first % 128:first + height].astype(F32).T[first % 128:].astype(BF16)
        side = jnp.where(half == fixed, 1, 0)
        if aligned:
            for d in range(count):
                out[side, d ^ me] = mm(n_t, dq_v[:, d * piece:(d + 1) * piece]).astype(BF16)
        else:
            out[side] = mm(n_t, dq_v[...]).astype(BF16)


def down_grad_call(chunk, chunks, count, tab, f, recv, cots, z):
    slots, rows, channels = f.shape
    width = z.shape[2] // 2 // chunks
    piece = channels // count
    aligned = piece % 16 == 0
    shape = (2, count, piece, width) if aligned else (2, channels, width)
    out = pl.pallas_call(
        functools.partial(down_grad_body, chunk, count, aligned),
        out_shape=jax.ShapeDtypeStruct(shape, BF16),
        in_specs=[IN_SMEM] + [IN_ANY] * 4,
        out_specs=IN_VMEM,
        scratch_shapes=[pltpu.VMEM((slots * rows, channels), BF16), pltpu.VMEM((2, slots * rows, width), BF16),
                        pltpu.SemaphoreType.DMA((slots,)), pltpu.SemaphoreType.DMA((2, slots))],
        compiler_params=pltpu.CompilerParams(vmem_limit_bytes=VMEM_BYTES),
        cost_estimate=pl.CostEstimate(flops=4 * slots * rows * channels * width, bytes_accessed=8 * channels * width, transcendentals=0),
        name="down_grad",
    )(tab, f, recv, cots, z)
    if not aligned:
        out = out.reshape(2, count, piece, width)[:, jnp.arange(count) ^ lax.axis_index("dp")]
    return out


def up_grad_call(chunk, chunks, count, tab, n, dq):
    slots, rows, channels = n.shape
    ff = dq.shape[2]
    height = channels // 2 // chunks
    piece = ff // count
    aligned = piece % 128 == 0
    shape = (2, count, height, piece) if aligned else (2, height, ff)
    out = pl.pallas_call(
        functools.partial(up_grad_body, chunk, count, aligned),
        out_shape=jax.ShapeDtypeStruct(shape, BF16),
        in_specs=[IN_SMEM] + [IN_ANY] * 2,
        out_specs=IN_VMEM,
        scratch_shapes=[pltpu.VMEM((slots * rows, channels), BF16), pltpu.VMEM((slots * rows, ff), BF16),
                        pltpu.SemaphoreType.DMA((slots,)), pltpu.SemaphoreType.DMA((slots,))],
        compiler_params=pltpu.CompilerParams(vmem_limit_bytes=VMEM_BYTES),
        cost_estimate=pl.CostEstimate(flops=4 * slots * rows * height * ff, bytes_accessed=8 * height * ff, transcendentals=0),
        name="up_grad",
    )(tab, n, dq)
    if not aligned:
        out = jnp.swapaxes(out.reshape(2, height, count, piece), 1, 2)[:, jnp.arange(count) ^ lax.axis_index("dp")]
    return out


def summed_pieces(pair, bits):
    other, mine = pair[0], pair[1]
    got = flipped(other, "pipe", 1)
    depth = len(bits)
    split = (2,) * depth + mine.shape[1:]
    mine = mine.reshape(split)
    got = got.reshape(split)
    axes = list(range(depth))[::-1]
    for bit in bits:
        axis = axes.index(bit)
        keep = [lax.index_in_dim(a, 0, axis, False) for a in (mine, got)]
        send = [lax.index_in_dim(a, 1, axis, False) for a in (mine, got)]
        sent = (send[0].astype(F32) + send[1].astype(F32)).astype(BF16)
        got = flipped(sent, "dp", 1 << bit)
        mine = (keep[0].astype(F32) + keep[1].astype(F32)).astype(BF16)
        axes.remove(bit)
    return mine.astype(F32) + got.astype(F32)


def join_body(half_ref, mine_up, got_up, mine_down, got_down, up_o, down_o, sems):
    half = half_ref[5, 1]
    copies = []
    for i, (mine, got, target) in enumerate(((mine_up, got_up, up_o), (mine_down, got_down, down_o))):
        size = mine.shape[0]
        own = pl.multiple_of(half * size, 16)
        rest = pl.multiple_of((1 - half) * size, 16)
        copies.append(pltpu.make_async_copy(mine, target.at[pl.ds(own, size), :], sems.at[i, 0]))
        copies.append(pltpu.make_async_copy(got, target.at[pl.ds(rest, size), :], sems.at[i, 1]))
    for copy in copies:
        copy.start()
    for copy in copies:
        copy.wait()


def place_body(route, low, high, mixed_o, grad_o, mixed_v, grad_v, sems):
    slots = low.shape[2]
    reads = []
    for place in range(2 * slots):
        source = (low, high)[place % 2]
        for kind, buffer in enumerate((mixed_v, grad_v)):
            image = route[2, place]
            copy = pltpu.make_async_copy(source.at[route[kind, place], kind, place // 2], buffer.at[image], sems.at[kind, place])
            copy.start()
            reads.append(copy)
    for copy in reads:
        copy.wait()
    writes = [pltpu.make_async_copy(mixed_v, mixed_o, sems.at[0, 0]), pltpu.make_async_copy(grad_v, grad_o, sems.at[1, 0])]
    for copy in writes:
        copy.start()
    for copy in writes:
        copy.wait()


def local(images, cotangent, valid_rows, skip_masks, norm_gain, norm_bias, token_up, token_up_bias, token_down,
          token_down_bias, chan_up, chan_up_bias, chan_down, chan_down_bias):
    count = lax.axis_size("dp")
    me = lax.axis_index("dp")
    section = lax.axis_index("pipe")
    half = section % 2
    layer = section // 2
    is_far = layer == 1
    is_first = half == 0
    patches = images.shape[1]
    channels = images.shape[2]
    rows = -(-patches // 16) * 16
    hidden_t = token_up.shape[1]

    own = (chan_up, chan_down, token_up, token_up_bias, token_down, token_down_bias, chan_up_bias, chan_down_bias, norm_gain, norm_bias)
    got = tuple(flipped(part, "pipe", 1) for part in own)

    def joined(i):
        return jnp.concatenate([jnp.where(is_first, own[i], got[i]), jnp.where(is_first, got[i], own[i])], 0)

    first_on = skip_masks[:, 0] * valid_rows
    second_on = skip_masks[:, 1] * valid_rows
    rank_class = jnp.where(first_on * second_on == 1, 0, jnp.where(second_on == 1, 1, jnp.where(first_on == 1, 2, 3)))
    slots_all = rank_class.shape[0]
    numbers = jnp.arange(slots_all)
    key = rank_class * slots_all + numbers
    place = jnp.sum(key[None, :] < key[:, None], axis=1)
    order = jnp.sum(jnp.where(place[None, :] == numbers[:, None], numbers[None, :], 0), axis=1).astype(jnp.int32)
    crossing = jnp.sum(first_on * second_on)
    hops = (crossing + 1) // 2

    own_order = jnp.where(is_first, order[0::2], order[1::2])
    first_here = first_on[own_order]
    second_here = second_on[own_order]
    valid_here = valid_rows[own_order]
    on_here = jnp.where(is_far, second_here, first_here)
    late = jnp.where(is_far, -1, hops - 1)
    tab = jnp.stack([on_here, valid_here, first_here * second_here, own_order, jnp.zeros_like(own_order),
                     jnp.stack([layer, half, me, late])]).astype(jnp.int32)

    up, down = pl.pallas_call(
        join_body,
        out_shape=[jax.ShapeDtypeStruct((2 * chan_up.shape[0], chan_up.shape[1]), BF16),
                   jax.ShapeDtypeStruct((2 * chan_down.shape[0], chan_down.shape[1]), BF16)],
        in_specs=[IN_SMEM] + [IN_ANY] * 4,
        out_specs=[IN_VMEM] * 2,
        scratch_shapes=[pltpu.SemaphoreType.DMA((2, 2))],
        compiler_params=pltpu.CompilerParams(vmem_limit_bytes=VMEM_BYTES),
        name="join",
    )(tab, chan_up, got[0], chan_down, got[1])

    def padded(array, axis):
        extra = [(0, 0)] * array.ndim
        extra[axis] = (0, rows - patches)
        return jnp.pad(array, extra)

    up_w = padded(joined(2), 0)
    down_w = padded(joined(4), 1)
    weights = {
        "up": up, "down": down,
        "up_w": up_w, "down_w": down_w,
        "up_t": up_w.T, "down_t": down_w.T,
        "up_col": joined(3).astype(F32)[:, None],
        "down_col": padded(joined(5).astype(F32), 0)[:, None],
        "u_row": joined(6).astype(F32)[None, :],
        "w_row": joined(7).astype(F32)[None, :],
        "gains": joined(8).astype(F32),
        "shifts": joined(9).astype(F32),
    }
    images_p = padded(images, 1)
    cots_p = padded(cotangent, 1)
    blank = images_p[0]

    def relay(length):
        def run(images_p, cots_p, tab, weights, blank):
            kept_f = [None] * 9
            kept_b = [None] * 7

            def forward(near, far, recv):
                out = forward_call((near, far), tab, images_p, recv, weights, kept_f)
                kept_f[:] = out
                kept_b[0] = out[0]

            def backward(near, far, recv):
                saved = (kept_f[3], kept_f[4], kept_f[5], kept_f[6], kept_f[7])
                out = backward_call((near, far), tab, cots_p, recv, weights, saved, kept_b)
                kept_b[:] = out
                kept_f[0] = out[0]

            def exchange():
                return flipped(kept_f[0], "pipe", 2)

            none = -1
            if length == 0:
                last = blank
                for slot in range(SLOTS):
                    forward(slot, slot, blank)
                    backward(slot, slot, blank)
            elif length == 1:
                forward(0, none, blank)
                x1 = exchange()
                forward(1, 1, blank)
                backward(1, 1, blank)
                forward(2, 0, x1)
                backward(2, 0, x1)
                x3 = exchange()
                forward(3, 2, blank)
                backward(3, 2, blank)
                forward(none, 3, blank)
                backward(none, 3, blank)
                last = x3
            elif length == 2:
                forward(0, none, blank)
                x1 = exchange()
                forward(1, 2, blank)
                backward(none, 2, blank)
                x2 = exchange()
                forward(2, 0, x1)
                backward(2, 0, x1)
                x3 = exchange()
                forward(3, 1, x2)
                backward(3, 1, x2)
                x4 = exchange()
                forward(none, 3, x3)
                backward(0, 3, x3)
                last = x4
            elif length == 3:
                forward(0, none, blank)
                x1 = exchange()
                forward(1, 3, blank)
                backward(none, 3, blank)
                x2 = exchange()
                forward(2, 0, x1)
                backward(none, 0, x1)
                x3 = exchange()
                forward(3, 1, x2)
                backward(3, 1, x2)
                x4 = exchange()
                forward(none, 2, x3)
                backward(0, 2, x3)
                x5 = exchange()
                backward(1, none, x4)
                last = x5
            else:
                forward(0, none, blank)
                x1 = exchange()
                forward(1, none, blank)
                x2 = exchange()
                forward(2, 0, x1)
                backward(none, 0, x1)
                x3 = exchange()
                forward(3, 1, x2)
                backward(none, 1, x2)
                x4 = exchange()
                forward(none, 2, x3)
                backward(0, 2, x3)
                x5 = exchange()
                forward(none, 3, x4)
                backward(1, 3, x4)
                x6 = exchange()
                backward(2, none, x5)
                last = x6
            return last, tuple(kept_f), tuple(kept_b)

        return run

    last, kept_f, kept_b = lax.switch(hops, [relay(n) for n in range(SLOTS + 1)], images_p, cots_p, tab, weights, blank)

    chunks = 2
    bits = list(range(count.bit_length() - 1))
    swapped_bits = [bits[1], bits[0]] + bits[2:]
    down_parts = [down_grad_call(chunk, chunks, count, tab, kept_b[2], last, cots_p, kept_f[2]) for chunk in range(chunks)]
    saved = (kept_f[3], kept_f[4], kept_f[5], kept_f[6], kept_f[7])
    kept_b = backward_call((None, -1), tab, cots_p, last, weights, saved, kept_b)
    up_parts = [up_grad_call(chunk, chunks, count, tab, kept_f[8], kept_b[3]) for chunk in range(chunks)]

    down_sums = [summed_pieces(part, swapped_bits if i == 0 else bits) for i, part in enumerate(down_parts)]
    up_sums = [summed_pieces(part, bits) for part in up_parts]
    chan_down_grad = jnp.concatenate([part.T for part in down_sums], 0)
    chan_up_grad = jnp.concatenate(up_sums, 0)

    live = (tab[ON] == 1)[:, None, None]
    da, db, vec = (jnp.sum(jnp.where(live, part, 0.0), axis=0) for part in kept_b[4:7])

    def halves(array):
        size = array.shape[0] // 2
        low, high = array[:size], array[size:]
        return jnp.where(is_first, low, high).reshape(-1), jnp.where(is_first, high, low).reshape(-1)

    ff = vec.shape[1]
    small = [halves(da[:patches]), halves(db[:, :patches]), halves(vec[6, :hidden_t]), halves(vec[7, :patches]),
             halves(vec[0]), halves(vec[1, :channels]), halves(vec[2:4, :channels]), halves(vec[4:6, :channels])]
    sizes = [pair[0].shape[0] for pair in small]
    padding = -sum(sizes) % 1024
    mine = jnp.concatenate([pair[0] for pair in small] + [jnp.zeros((padding,), F32)])
    theirs = jnp.concatenate([pair[1] for pair in small] + [jnp.zeros((padding,), F32)]).astype(BF16)
    total = mine + flipped(theirs, "pipe", 1).astype(F32)
    for bit in bits:
        sent = lax.optimization_barrier(total.astype(BF16))
        total = sent.astype(F32) + flipped(sent, "dp", 1 << bit).astype(F32)
    pieces = []
    start = 0
    for size in sizes:
        pieces.append(total[start:start + size])
        start += size

    width = channels // lax.axis_size("pipe")
    result = jnp.stack([kept_f[1], kept_b[1]])[:, :, :patches]

    def slab(flip):
        return lax.dynamic_slice_in_dim(result, (section ^ flip) * width, width, 3)

    here = slab(0)
    beside, across, corner = (flipped(slab(flip), "pipe", flip) for flip in (1, 2, 3))

    def by_layer(own_layer, other_layer):
        return jnp.where(is_far, jnp.stack([other_layer, own_layer]), jnp.stack([own_layer, other_layer]))

    low = by_layer(jnp.where(is_first, here, beside), jnp.where(is_first, across, corner))
    high = by_layer(jnp.where(is_first, beside, here), jnp.where(is_first, corner, across))
    only_first = first_on * (1 - second_on)
    only_second = second_on * (1 - first_on)
    route = jnp.stack([1 - only_first[order], only_second[order], order]).astype(jnp.int32)
    out_shape = jax.ShapeDtypeStruct((images.shape[0], patches, width), BF16)
    mixed, input_grad = pl.pallas_call(
        place_body,
        out_shape=[out_shape, out_shape],
        in_specs=[IN_SMEM] + [IN_ANY] * 2,
        out_specs=[IN_ANY] * 2,
        scratch_shapes=[pltpu.VMEM(out_shape.shape, BF16), pltpu.VMEM(out_shape.shape, BF16), pltpu.SemaphoreType.DMA((2, 2 * SLOTS))],
        compiler_params=pltpu.CompilerParams(vmem_limit_bytes=VMEM_BYTES),
        name="place",
    )(route, low, high)

    return (
        mixed,
        input_grad,
        pieces[6][None, :],
        pieces[7][None, :],
        pieces[0].reshape(token_up.shape),
        pieces[2],
        pieces[1].reshape(token_down.shape),
        pieces[3],
        chan_up_grad,
        pieces[4],
        chan_down_grad,
        pieces[5],
    )


def solution(mesh):
    placed = (
        P("dp", None, None),
        P("dp", None, None),
        P("dp"),
        P("dp", None),
        P("pipe", None),
        P("pipe", None),
        P("pipe", None),
        P("pipe"),
        P("pipe", None),
        P("pipe"),
        P("pipe", None),
        P("pipe"),
        P("pipe", None),
        P("pipe"),
    )
    return jax.shard_map(
        local,
        mesh=mesh,
        in_specs=placed,
        out_specs=(
            P("dp", None, "pipe"),
            P("dp", None, "pipe"),
            P("pipe", None),
            P("pipe", None),
            P("pipe", None),
            P("pipe"),
            P("pipe", None),
            P("pipe"),
            P("pipe", "dp"),
            P("pipe"),
            P("pipe", "dp"),
            P("pipe"),
        ),
        check_vma=False,
    )
```

time: 892 us -> 379 us (0.42); the launches traced: 885 us -> 382 us
  waiting for transfers between devices: 306 us -> 80.6 us
  other arithmetic: 184 us -> 38.2 us
  local copies, waits for them, and re-layouts: 188 us -> 52.9 us
  Pallas kernels: 0 us -> 94.9 us
  matrix products: 47.8 us -> 0 us
  starting transfers between devices: 35 us -> 79 us
  blocking collectives: 39.6 us -> 0 us
  loops' own time: 68.8 us -> 34.3 us
  between operations: 16.3 us -> 2.43 us
    reduce_scatter x4 -> x0, waiting for transfers between devices: 158 us -> none  [the longest x1 99.5 us: local(): lax.psum_scatter(joined[4], 'dp', scatter_dimension=1, tiled=True)]
    pallas_call x0 -> x17, Pallas kernels: none -> 94.9 us  [the longest x11 61.5 us: kept_call(): pl.pallas_call(trimmed, out_shape=shapes, in_specs=specs + [IN_ANY] * pas...]
    dynamic_update_slice x14 -> x0, other arithmetic: 85.6 us -> none  [store_slot(): return lax.dynamic_update_index_in_dim(buffer, chosen, slot_index, 0)]
    ppermute x24 -> x38, waiting for transfers between devices: 148 us -> 80.6 us  [flipped(): return lax.ppermute(block, axis, route)]
    dynamic_slice x22 -> x3, local copies, waits for them, and re-layouts: 70.7 us -> 6.75 us  [slab(): return lax.dynamic_slice_in_dim(result, (section ^ flip) * width, width, 3)]
    dot_general x12 -> x0, matrix products: 47.8 us -> none  [the longest x2 14.6 us: token_back(): jnp.einsum('bpd,tp->bdt', grad_branch, weights[2], preferred_element_type...]
    ppermute x24 -> x38, starting transfers between devices: 34.8 us -> 79 us  [flipped(): return lax.ppermute(block, axis, route)]
    another operation x20 -> x8, local copies, waits for them, and re-layouts: 40.3 us -> 0.59 us
  transfers between devices with their start and end apart: 29 -> 38, of which waited for: 13 -> 17; matrix products, arithmetic and copies ran while one was open for 32% -> 21% of each run, Pallas kernels for 0% -> 4%
where the time goes in v1:
time: 379 us; the launch traced here: 382 us
  Pallas kernels  94.9 us (25%)
  waiting for transfers between devices  80.6 us (21%)
  starting transfers between devices  79 us (21%)
  local copies, waits for them, and re-layouts  52.9 us (14%)
  other arithmetic  38.2 us (10%)
  loops' own time  34.3 us (9%)
    ppermute x38, waiting for transfers between devices, flipped(): return lax.ppermute(block, axis, route)  80.6 us
    ppermute x38, starting transfers between devices, flipped(): return lax.ppermute(block, axis, route)  79 us
    pallas_call x11, Pallas kernels, kept_call(): pl.pallas_call(trimmed, out_shape=shapes, in_specs=specs + [IN_ANY] * pas...  61.5 us
    another operation x1, loops' own time, local(): lax.switch(hops, [relay(n) for n in range(SLOTS + 1)], images_p, cots_p,...  34.3 us
    convert_element_type x8, other arithmetic, summed_pieces(): mine = (keep[0].astype(F32) + keep[1].astype(F32)).astype(BF16)  14.3 us
    pallas_call x2, Pallas kernels, up_grad_call(): pl.pallas_call(functools.partial(up_grad_body, chunk, count, aligned), ou...  12.8 us
    pallas_call x2, Pallas kernels, down_grad_call(): pl.pallas_call(functools.partial(down_grad_body, chunk, count, aligned),...  10.5 us
    unnamed x58, local copies, waits for them, and re-layouts  8.76 us
  transfers between devices with their start and end apart: 38, of which 17 were waited for; matrix products, arithmetic and copies ran while one was open for 21% of the time, Pallas kernels for 4%

profile of v1, /device:TPU:0, one launch (start us, length us, event | category | flops | bytes accessed | tf_op | source)
XLA Modules:
  0.0 382.3 jit_solution(16684049215054663051)
XLA Ops:
  22.9 6.9 %join.1 = (bf16[768,3072]{1,0:T(8,128)(2,1)}, bf16[3072,768]{1,0:T(8,128)(2,1)}) custom-call(s32[6,4]{1,0:T(8,128)S(1)} %stack.87.half_ref.refs_0_.tab, bf16[384,3072]{1,0:T(8,128)(2,1)S(1)} %copy-done, bf16[384,3072]{1,0:T(8,128)(2,1)} %collective-permute-done.17.got_up, bf16[1536,768]{1,0:T(8,128)(2,1)S(1)} %copy-done.1, ...), custom_call_target="tpu_custom_call" | custom-call | tf_op jit(solution)/shard_map/join/pallas_call | solution.py:557
  29.9 163.2 %conditional.1 = (bf16[208,768]{1,0:T(8,128)(2,1)}, bf16[4,208,768]{2,1,0:T(8,128)(2,1)}, bf16[4,208,3072]{2,1,0:T(8,128)(2,1)}, bf16[4,208,3072]{2,1,0:T(8,128)...) conditional(s32[]{:T(128)} %clamp.3, (s32[6,4]{1,0:T(8,128)S(1)}, ...), branch_computations={%region_3.4_spmd, %region_4.5_spmd, %region_5.6_spmd, %region_6.7_... | conditional | flops 25518145536 | bytes 113939616 | solution.py:683
  50.2 12.2 %forward_slot.39 = (bf16[208,768]{1,0:T(8,128)(2,1)}, bf16[4,208,768]{2,1,0:T(8,128)(2,1)}, bf16[4,208,3072]{2,1,0:T(8,128)(2,1)}, bf16[4,208,3072]{2,1,0:T(8,12...) custom-call(s32[6,4]{1,0:T(8,128)S(1)} %get-tuple-element.418.refs_0, ...), custom_call_target="tpu_custom_call" | custom-call | flops 2208301056 | bytes 5111808 | tf_op jit(solution)/shard_map/cond/branch_3_fun/forward_slot/pallas_call | solution.py:260
  62.5 9.8 %collective-permute-done.6.refs_2_ = bf16[208,768]{1,0:T(8,128)(2,1)S(1)} collective-permute-done((bf16[208,768]{1,0:T(8,128)(2,1)}, bf16[208,768]{1,0:T(8,128)(2,1)S(1)}, u32[]{:S(2)}, u32[]{:S(2)}) %collective-permute-start.6) | collective-permute-done | bytes 319520 | tf_op jit(solution)/shard_map/cond/branch_3_fun/ppermute | solution.py:29
  72.4 9.7 %forward_slot.40 = (bf16[208,768]{1,0:T(8,128)(2,1)}, bf16[4,208,768]{2,1,0:T(8,128)(2,1)}, bf16[4,208,3072]{2,1,0:T(8,128)(2,1)}, bf16[4,208,3072]{2,1,0:T(8,12...) custom-call(s32[6,4]{1,0:T(8,128)S(1)} %get-tuple-element.418.refs_0, ...), custom_call_target="tpu_custom_call", output_to_operand_aliasing={{0}: (13, {}), {1}: (14, {}), {2}: (15, {}), {3}: (16, {}),... | custom-call | flops 2208301056 | bytes 5111808 | tf_op jit(solution)/shard_map/cond/branch_3_fun/forward_slot/pallas_call | solution.py:260
  83.1 7.9 %collective-permute-start.8 = (bf16[208,768]{1,0:T(8,128)(2,1)}, bf16[208,768]{1,0:T(8,128)(2,1)S(1)}, u32[]{:S(2)}, u32[]{:S(2)}) collective-permute-start(bf16[208,768]{1,0:T(8,128)(2,1)} %get-tuple-element.449.refs_13_), channel_id=1, source_target_pairs={{0,2},{1,3},{2,0},{3,1},{4,6},{5,7},{6,4},{7,5},{8,10},{9,11},{10,... | collective-permute-start | bytes 958472 | tf_op jit(solution)/shard_map/cond/branch_3_fun/ppermute | solution.py:29
  91.0 7.6 %collective-permute-done.8.refs_2_ = bf16[208,768]{1,0:T(8,128)(2,1)S(1)} collective-permute-done((bf16[208,768]{1,0:T(8,128)(2,1)}, bf16[208,768]{1,0:T(8,128)(2,1)S(1)}, u32[]{:S(2)}, u32[]{:S(2)}) %collective-permute-start.8) | collective-permute-done | bytes 319520 | tf_op jit(solution)/shard_map/cond/branch_3_fun/ppermute | solution.py:29
  98.6 7.8 %forward_slot.41 = (bf16[208,768]{1,0:T(8,128)(2,1)}, bf16[4,208,768]{2,1,0:T(8,128)(2,1)}, bf16[4,208,3072]{2,1,0:T(8,128)(2,1)}, bf16[4,208,3072]{2,1,0:T(8,12...) custom-call(s32[6,4]{1,0:T(8,128)S(1)} %get-tuple-element.418.refs_0, ...), custom_call_target="tpu_custom_call", output_to_operand_aliasing={{0}: (13, {}), {1}: (14, {}), {2}: (15, {}), {3}: (16, {}),... | custom-call | flops 2208301056 | bytes 5111808 | tf_op jit(solution)/shard_map/cond/branch_3_fun/forward_slot/pallas_call | solution.py:260
  107.6 8.9 %collective-permute-start.7 = (bf16[208,768]{1,0:T(8,128)(2,1)}, bf16[208,768]{1,0:T(8,128)(2,1)S(1)}, u32[]{:S(2)}, u32[]{:S(2)}) collective-permute-start(bf16[208,768]{1,0:T(8,128)(2,1)} %get-tuple-element.465.refs_13_), channel_id=1, source_target_pairs={{0,2},{1,3},{2,0},{3,1},{4,6},{5,7},{6,4},{7,5},{8,10},{9,11},{10,... | collective-permute-start | bytes 958472 | tf_op jit(solution)/shard_map/cond/branch_3_fun/ppermute | solution.py:29
  116.5 6.7 %collective-permute-done.7.refs_2_ = bf16[208,768]{1,0:T(8,128)(2,1)S(1)} collective-permute-done((bf16[208,768]{1,0:T(8,128)(2,1)}, bf16[208,768]{1,0:T(8,128)(2,1)S(1)}, u32[]{:S(2)}, u32[]{:S(2)}) %collective-permute-start.7) | collective-permute-done | bytes 319520 | tf_op jit(solution)/shard_map/cond/branch_3_fun/ppermute | solution.py:29
  126.6 14.5 %collective-permute-start.10 = (bf16[208,768]{1,0:T(8,128)(2,1)}, bf16[208,768]{1,0:T(8,128)(2,1)S(1)}, u32[]{:S(2)}, u32[]{:S(2)}) collective-permute-start(bf16[208,768]{1,0:T(8,128)(2,1)} %get-tuple-element.481.refs_13_), channel_id=1, source_target_pairs={{0,2},{1,3},{2,0},{3,1},{4,6},{5,7},{6,4},{7,5},{8,10},{9,11},{10,... | collective-permute-start | bytes 958472 | tf_op jit(solution)/shard_map/cond/branch_3_fun/ppermute | solution.py:29
  141.2 5.8 %collective-permute-done.10.refs_2_ = bf16[208,768]{1,0:T(8,128)(2,1)S(1)} collective-permute-done((bf16[208,768]{1,0:T(8,128)(2,1)}, bf16[208,768]{1,0:T(8,128)(2,1)S(1)}, u32[]{:S(2)}, u32[]{:S(2)}) %collective-permute-start.10) | collective-permute-done | bytes 319520 | tf_op jit(solution)/shard_map/cond/branch_3_fun/ppermute | solution.py:29
  147.7 8.6 %backward_slot.38 = (bf16[208,768]{1,0:T(8,128)(2,1)}, bf16[4,208,768]{2,1,0:T(8,128)(2,1)}, bf16[4,208,768]{2,1,0:T(8,128)(2,1)}, bf16[4,208,3072]{2,1,0:T(8,12...) custom-call(s32[6,4]{1,0:T(8,128)S(1)} %get-tuple-element.418.refs_0, ...), custom_call_target="tpu_custom_call", output_to_operand_aliasing={{0}: (14, {}), {1}: (15, {}), {2}: (16, {}), {3}: (17, {}),... | custom-call | flops 2453667840 | bytes 5111808 | tf_op jit(solution)/shard_map/cond/branch_3_fun/backward_slot/pallas_call | solution.py:260
  156.2 8.7 %collective-permute-start.9 = (bf16[208,768]{1,0:T(8,128)(2,1)}, bf16[208,768]{1,0:T(8,128)(2,1)}, u32[]{:S(2)}, u32[]{:S(2)}) collective-permute-start(bf16[208,768]{1,0:T(8,128)(2,1)} %get-tuple-element.497.refs_14_), channel_id=1, source_target_pairs={{0,2},{1,3},{2,0},{3,1},{4,6},{5,7},{6,4},{7,5},{8,10},{9,11},{10,... | collective-permute-start | bytes 958472 | tf_op jit(solution)/shard_map/cond/branch_3_fun/ppermute | solution.py:29
  164.9 5.3 %collective-permute-done.9 = bf16[208,768]{1,0:T(8,128)(2,1)} collective-permute-done((bf16[208,768]{1,0:T(8,128)(2,1)}, bf16[208,768]{1,0:T(8,128)(2,1)}, u32[]{:S(2)}, u32[]{:S(2)}) %collective-permute-start.9) | collective-permute-done | bytes 319520 | tf_op jit(solution)/shard_map/cond/branch_3_fun/ppermute | solution.py:29
  170.2 8.5 %backward_slot.39 = (bf16[208,768]{1,0:T(8,128)(2,1)}, bf16[4,208,768]{2,1,0:T(8,128)(2,1)}, bf16[4,208,768]{2,1,0:T(8,128)(2,1)}, bf16[4,208,3072]{2,1,0:T(8,12...) custom-call(s32[6,4]{1,0:T(8,128)S(1)} %get-tuple-element.418.refs_0, ...), custom_call_target="tpu_custom_call", output_to_operand_aliasing={{0}: (14, {}), {1}: (15, {}), {2}: (16, {}), {3}: (17, {}),... | custom-call | flops 2453667840 | bytes 5111808 | tf_op jit(solution)/shard_map/cond/branch_3_fun/backward_slot/pallas_call | solution.py:260
  193.1 5.4 %down_grad.2 = bf16[2,8,96,768]{3,2,1,0:T(8,128)(2,1)S(1)} custom-call(s32[6,4]{1,0:T(8,128)S(1)} %stack.87.half_ref.refs_0_.tab, bf16[4,208,768]{2,1,0:T(8,128)(2,1)} %get-tuple-element.667.refs_16_.f_i, bf16[208,768]{1,0:T(8,128)(2,1)} %get-tuple-element.659.refs_2_.recv, bf16[8,208,768]{2,1,0:T(8,128)(2,1)} %pad.24.refs_1_.cots, ...), custom_call_target="tpu_custom_call" | custom-call | flops 1962934272 | bytes 4718592 | tf_op jit(solution)/shard_map/down_grad/pallas_call | solution.py:425
  198.6 5.1 %down_grad.3 = bf16[2,8,96,768]{3,2,1,0:T(8,128)(2,1)S(1)} custom-call(s32[6,4]{1,0:T(8,128)S(1)} %stack.87.half_ref.refs_0_.tab, bf16[4,208,768]{2,1,0:T(8,128)(2,1)} %get-tuple-element.667.refs_16_.f_i, bf16[208,768]{1,0:T(8,128)(2,1)} %get-tuple-element.659.refs_2_.recv, bf16[8,208,768]{2,1,0:T(8,128)(2,1)S(1)} %copy-done.7, ...), custom_call_target="tpu_custom_call" | custom-call | flops 1962934272 | bytes 4718592 | tf_op jit(solution)/shard_map/down_grad/pallas_call | solution.py:425
  206.2 8.4 %backward_slot.45 = (bf16[208,768]{1,0:T(8,128)(2,1)}, bf16[4,208,768]{2,1,0:T(8,128)(2,1)}, bf16[4,208,768]{2,1,0:T(8,128)(2,1)}, bf16[4,208,3072]{2,1,0:T(8,12...) custom-call(s32[6,4]{1,0:T(8,128)S(1)} %stack.87.half_ref.refs_0_.ta, ...), custom_call_target="tpu_custom_call", output_to_operand_aliasing={{0}: (14, {}), {1}: (15, {}), {2}: (16, {}), {3}: (17, {}),... | custom-call | flops 2453667840 | bytes 5111808 | tf_op jit(solution)/shard_map/backward_slot/pallas_call | solution.py:260
  220.3 7.6 %concatenate.85 = bf16[79872]{0:T(1024)(128)(2,1)} concatenate(bf16[37632]{0:T(1024)(128)(2,1)S(1)} %reshape.379, bf16[37632]{0:T(1024)(128)(2,1)S(1)} %reshape.380, bf16[192]{0:T(256)(128)(2,1)S(1)} %fusion.53, bf16[98]{0:T(256)(128)(2,1)S(1)} %fusion.58, bf16[1536]{0:T(1024)(128)(2,1)S(1)} %fusion.42, bf16[384]{0:T(512)(128)(2,1)S(1)} %fusion.51, ...), dimensions={0} | concatenate | bytes 319488 | tf_op jit(solution)/shard_map/concatenate | solution.py:712
  228.0 6.4 %up_grad.2 = bf16[2,8,192,384]{3,2,1,0:T(8,128)(2,1)S(1)} custom-call(s32[6,4]{1,0:T(8,128)S(1)} %stack.87.half_ref.refs_0_.tab, bf16[4,208,768]{2,1,0:T(8,128)(2,1)} %get-tuple-element.678.n_i, bf16[4,208,3072]{2,1,0:T(8,128)(2,1)} %get-tuple-element.679.dq_i), custom_call_target="tpu_custom_call" | custom-call | flops 1962934272 | bytes 4718592 | tf_op jit(solution)/shard_map/up_grad/pallas_call | solution.py:448
  238.4 18.9 %collective-permute-start.31 = (bf16[79872]{0:T(1024)(128)(2,1)S(1)}, bf16[79872]{0:T(1024)(128)(2,1)S(1)}, u32[]{:S(2)}, u32[]{:S(2)}) collective-permute-start(bf16[79872]{0:T(1024)(128)(2,1)S(1)} %add_convert_fusion.18), channel_id=1, source_target_pairs={{0,4},{4,0},{8,12},{12,8},{16,20},{20,16},{24,28},{28,24},{1,5},{5... | collective-permute-start | bytes 479240 | tf_op jit(solution)/shard_map/ppermute | solution.py:29
  257.3 6.4 %up_grad.3 = bf16[2,8,192,384]{3,2,1,0:T(8,128)(2,1)S(1)} custom-call(s32[6,4]{1,0:T(8,128)S(1)} %stack.87.half_ref.refs_0_.tab, bf16[4,208,768]{2,1,0:T(8,128)(2,1)} %get-tuple-element.678.n_i, bf16[4,208,3072]{2,1,0:T(8,128)(2,1)} %get-tuple-element.679.dq_i), custom_call_target="tpu_custom_call" | custom-call | flops 1962934272 | bytes 4718592 | tf_op jit(solution)/shard_map/up_grad/pallas_call | solution.py:448
  275.7 6.3 %select_bitcast_fusion = (bf16[1,2,4,196,192]{4,3,2,1,0:T(8,128)(2,1)}, bf16[1,2,4,196,192]{4,3,2,1,0:T(8,128)(2,1)}, bf16[2,4,196,192]{3,2,1,0:T(8,128)(2,1)}, bf16[2,4,196,192]{3,2,1,0:T(8,128)(2,1)}) fusion(bf16[2,4,196,192]{3,2,1,0:T(8,128)(2,1)} %copy.483, pred[]{:T(512)S(6)} %eq.44, s32[]{:T(128)S(6)} %select_n.378, ...), kind=kLoop, calls=%fused_computation.33 | loop fusion | flops 5419008 | bytes 5566477 | tf_op jit(solution)/shard_map/stack | solution.py:733
  314.5 8.8 %collective-permute-done.28 = bf16[2,4,196,192]{2,3,1,0:T(8,128)(2,1)} collective-permute-done((bf16[2,4,196,192]{2,3,1,0:T(8,128)(2,1)}, bf16[2,4,196,192]{2,3,1,0:T(8,128)(2,1)}, u32[]{:S(2)}, u32[]{:S(2)}) %collective-permute-start.28) | collective-permute-done | bytes 602144 | tf_op jit(solution)/shard_map/ppermute | solution.py:29
  327.5 3.1 place.1
  339.7 7.3 %collective-permute-done.39 = bf16[2,2,192,384]{3,2,1,0:T(8,128)(2,1)S(1)} collective-permute-done((bf16[2,2,192,384]{3,2,1,0:T(8,128)(2,1)}, bf16[2,2,192,384]{3,2,1,0:T(8,128)(2,1)S(1)}, u32[]{:S(2)}, u32[]{:S(2)}) %collective-permute-start.39) | collective-permute-done | bytes 589856 | tf_op jit(solution)/shard_map/ppermute | solution.py:29
  347.3 5.0 %collective-permute-done.44 = bf16[2,96,768]{2,1,0:T(8,128)(2,1)S(1)} collective-permute-done((bf16[2,96,768]{2,1,0:T(8,128)(2,1)S(1)}, bf16[2,96,768]{2,1,0:T(8,128)(2,1)S(1)}, u32[]{:S(2)}, u32[]{:S(2)}) %collective-permute-start.44) | collective-permute-done | bytes 294944 | tf_op jit(solution)/shard_map/ppermute | solution.py:29
  352.3 3.0 collective-permute-start.45
  355.5 3.0 collective-permute-start.37
  358.5 4.6 %collective-permute-done.40 = bf16[2,192,384]{2,1,0:T(8,128)(2,1)S(1)} collective-permute-done((bf16[2,192,384]{2,1,0:T(8,128)(2,1)S(1)}, bf16[2,192,384]{2,1,0:T(8,128)(2,1)S(1)}, u32[]{:S(2)}, u32[]{:S(2)}) %collective-permute-start.40) | collective-permute-done | bytes 294944 | tf_op jit(solution)/shard_map/ppermute | solution.py:29
  364.0 11.7 %collective-permute-done.49 = bf16[96,768]{1,0:T(8,128)(2,1)S(1)} collective-permute-done((bf16[96,768]{1,0:T(8,128)(2,1)S(1)}, bf16[96,768]{1,0:T(8,128)(2,1)S(1)}, u32[]{:S(2)}, u32[]{:S(2)}) %collective-permute-start.49) | collective-permute-done | bytes 147488 | tf_op jit(solution)/shard_map/ppermute | solution.py:29
  (260 shorter events, 105.6 us)
Async XLA Ops:
  0.7 20.6 %collective-permute-start.17 = (bf16[384,3072]{1,0:T(8,128)(2,1)}, bf16[384,3072]{1,0:T(8,128)(2,1)}, u32[]{:S(2)}, u32[]{:S(2)}) collective-permute-start(bf16[384,3072]{1,0:T(8,128)(2,1)} %mine_up.1), channel_id=1, source_target_pairs={{0,1},{1,0},{2,3},{3,2},{4,5},{5,4},{6,7},{7,6},{8,9},{9,8},{10,11... | collective-permute-start | bytes 7077896 | tf_op jit(solution)/shard_map/ppermute | solution.py:29
  1.2 20.1 %collective-permute-start.18 = (bf16[1536,768]{1,0:T(8,128)(2,1)}, bf16[1536,768]{1,0:T(8,128)(2,1)}, u32[]{:S(2)}, u32[]{:S(2)}) collective-permute-start(bf16[1536,768]{1,0:T(8,128)(2,1)} %mine_down.1), channel_id=1, source_target_pairs={{0,1},{1,0},{2,3},{3,2},{4,5},{5,4},{6,7},{7,6},{8,9},{9,8},{10,11... | collective-permute-start | bytes 7077896 | tf_op jit(solution)/shard_map/ppermute | solution.py:29
  1.3 19.9 %collective-permute-start.20 = (bf16[192,196]{1,0:T(8,128)(2,1)}, bf16[192,196]{1,0:T(8,128)(2,1)S(1)}, u32[]{:S(2)}, u32[]{:S(2)}) collective-permute-start(bf16[192,196]{1,0:T(8,128)(2,1)} %param.27), channel_id=1, source_target_pairs={{0,1},{1,0},{2,3},{3,2},{4,5},{5,4},{6,7},{7,6},{8,9},{9,8},{10,11... | collective-permute-start | bytes 225800 | tf_op jit(solution)/shard_map/ppermute | solution.py:29
  1.7 16.6 %collective-permute-start.25 = (bf16[1,768]{1,0:T(2,128)(2,1)}, bf16[1,768]{1,0:T(2,128)(2,1)S(1)}, u32[]{:S(2)}, u32[]{:S(2)}) collective-permute-start(bf16[1,768]{1,0:T(2,128)(2,1)} %param.23), channel_id=1, source_target_pairs={{0,1},{1,0},{2,3},{3,2},{4,5},{5,4},{6,7},{7,6},{8,9},{9,8},{10,11... | collective-permute-start | bytes 4616 | tf_op jit(solution)/shard_map/ppermute | solution.py:29
  1.8 13.9 %collective-permute-start.22 = (bf16[98]{0:T(256)(128)(2,1)}, bf16[98]{0:T(256)(128)(2,1)S(1)}, u32[]{:S(2)}, u32[]{:S(2)}) collective-permute-start(bf16[98]{0:T(256)(128)(2,1)} %param.28), channel_id=1, source_target_pairs={{0,1},{1,0},{2,3},{3,2},{4,5},{5,4},{6,7},{7,6},{8,9},{9,8},{10,11... | collective-permute-start | bytes 596 | tf_op jit(solution)/shard_map/ppermute | solution.py:29
  62.4 9.9 %collective-permute-start.6 = (bf16[208,768]{1,0:T(8,128)(2,1)}, bf16[208,768]{1,0:T(8,128)(2,1)S(1)}, u32[]{:S(2)}, u32[]{:S(2)}) collective-permute-start(bf16[208,768]{1,0:T(8,128)(2,1)} %get-tuple-element.432.refs_13_), channel_id=1, source_target_pairs={{0,2},{1,3},{2,0},{3,1},{4,6},{5,7},{6,4},{7,5},{8,10},{9,11},{10,... | collective-permute-start | bytes 958472 | tf_op jit(solution)/shard_map/cond/branch_3_fun/ppermute | solution.py:29
  83.1 15.5 %collective-permute-start.8 = (bf16[208,768]{1,0:T(8,128)(2,1)}, bf16[208,768]{1,0:T(8,128)(2,1)S(1)}, u32[]{:S(2)}, u32[]{:S(2)}) collective-permute-start(bf16[208,768]{1,0:T(8,128)(2,1)} %get-tuple-element.449.refs_13_), channel_id=1, source_target_pairs={{0,2},{1,3},{2,0},{3,1},{4,6},{5,7},{6,4},{7,5},{8,10},{9,11},{10,... | collective-permute-start | bytes 958472 | tf_op jit(solution)/shard_map/cond/branch_3_fun/ppermute | solution.py:29
  107.6 15.6 %collective-permute-start.7 = (bf16[208,768]{1,0:T(8,128)(2,1)}, bf16[208,768]{1,0:T(8,128)(2,1)S(1)}, u32[]{:S(2)}, u32[]{:S(2)}) collective-permute-start(bf16[208,768]{1,0:T(8,128)(2,1)} %get-tuple-element.465.refs_13_), channel_id=1, source_target_pairs={{0,2},{1,3},{2,0},{3,1},{4,6},{5,7},{6,4},{7,5},{8,10},{9,11},{10,... | collective-permute-start | bytes 958472 | tf_op jit(solution)/shard_map/cond/branch_3_fun/ppermute | solution.py:29
  126.6 20.3 %collective-permute-start.10 = (bf16[208,768]{1,0:T(8,128)(2,1)}, bf16[208,768]{1,0:T(8,128)(2,1)S(1)}, u32[]{:S(2)}, u32[]{:S(2)}) collective-permute-start(bf16[208,768]{1,0:T(8,128)(2,1)} %get-tuple-element.481.refs_13_), channel_id=1, source_target_pairs={{0,2},{1,3},{2,0},{3,1},{4,6},{5,7},{6,4},{7,5},{8,10},{9,11},{10,... | collective-permute-start | bytes 958472 | tf_op jit(solution)/shard_map/cond/branch_3_fun/ppermute | solution.py:29
  156.2 14.0 %collective-permute-start.9 = (bf16[208,768]{1,0:T(8,128)(2,1)}, bf16[208,768]{1,0:T(8,128)(2,1)}, u32[]{:S(2)}, u32[]{:S(2)}) collective-permute-start(bf16[208,768]{1,0:T(8,128)(2,1)} %get-tuple-element.497.refs_14_), channel_id=1, source_target_pairs={{0,2},{1,3},{2,0},{3,1},{4,6},{5,7},{6,4},{7,5},{8,10},{9,11},{10,... | collective-permute-start | bytes 958472 | tf_op jit(solution)/shard_map/cond/branch_3_fun/ppermute | solution.py:29
  219.5 76.7 %collective-permute-start.42 = (bf16[8,96,768]{2,1,0:T(8,128)(2,1)}, bf16[8,96,768]{2,1,0:T(8,128)(2,1)}, u32[]{:S(2)}, u32[]{:S(2)}) collective-permute-start(bf16[8,96,768]{2,1,0:T(8,128)(2,1)} %get-tuple-element.1063), channel_id=1, source_target_pairs={{0,1},{1,0},{2,3},{3,2},{4,5},{5,4},{6,7},{7,6},{8,9},{9,8},{10,11... | collective-permute-start | bytes 3538952 | tf_op jit(solution)/shard_map/ppermute | solution.py:29
  219.5 81.2 %collective-permute-start.46 = (bf16[8,96,768]{2,1,0:T(8,128)(2,1)}, bf16[8,96,768]{2,1,0:T(8,128)(2,1)}, u32[]{:S(2)}, u32[]{:S(2)}) collective-permute-start(bf16[8,96,768]{2,1,0:T(8,128)(2,1)} %get-tuple-element.1067), channel_id=1, source_target_pairs={{0,1},{1,0},{2,3},{3,2},{4,5},{5,4},{6,7},{7,6},{8,9},{9,8},{10,11... | collective-permute-start | bytes 3538952 | tf_op jit(solution)/shard_map/ppermute | solution.py:29
  227.9 10.4 %collective-permute-start.30 = (bf16[79872]{0:T(1024)(128)(2,1)}, bf16[79872]{0:T(1024)(128)(2,1)S(1)}, u32[]{:S(2)}, u32[]{:S(2)}) collective-permute-start(bf16[79872]{0:T(1024)(128)(2,1)} %concatenate.85), channel_id=1, source_target_pairs={{0,1},{1,0},{2,3},{3,2},{4,5},{5,4},{6,7},{7,6},{8,9},{9,8},{10,11... | collective-permute-start | bytes 479240 | tf_op jit(solution)/shard_map/ppermute | solution.py:29
  236.0 69.3 %collective-permute-start.34 = (bf16[8,192,384]{2,1,0:T(8,128)(2,1)}, bf16[8,192,384]{2,1,0:T(8,128)(2,1)}, u32[]{:S(2)}, u32[]{:S(2)}) collective-permute-start(bf16[8,192,384]{2,1,0:T(8,128)(2,1)} %get-tuple-element.1071), channel_id=1, source_target_pairs={{0,1},{1,0},{2,3},{3,2},{4,5},{5,4},{6,7},{7,6},{8,9},{9,8},{10,11... | collective-permute-start | bytes 3538952 | tf_op jit(solution)/shard_map/ppermute | solution.py:29
  238.4 25.4 %collective-permute-start.31 = (bf16[79872]{0:T(1024)(128)(2,1)S(1)}, bf16[79872]{0:T(1024)(128)(2,1)S(1)}, u32[]{:S(2)}, u32[]{:S(2)}) collective-permute-start(bf16[79872]{0:T(1024)(128)(2,1)S(1)} %add_convert_fusion.18), channel_id=1, source_target_pairs={{0,4},{4,0},{8,12},{12,8},{16,20},{20,16},{24,28},{28,24},{1,5},{5... | collective-permute-start | bytes 479240 | tf_op jit(solution)/shard_map/ppermute | solution.py:29
  264.5 6.3 %collective-permute-start.32 = (bf16[79872]{0:T(1024)(128)(2,1)}, bf16[79872]{0:T(1024)(128)(2,1)}, u32[]{:S(2)}, u32[]{:S(2)}) collective-permute-start(bf16[79872]{0:T(1024)(128)(2,1)} %add_convert_fusion.17), channel_id=1, source_target_pairs={{0,8},{4,12},{8,0},{12,4},{16,24},{20,28},{24,16},{28,20},{1,9},{5... | collective-permute-start | bytes 479240 | tf_op jit(solution)/shard_map/ppermute | solution.py:29
  265.7 42.7 %collective-permute-start.38 = (bf16[8,192,384]{2,1,0:T(8,128)(2,1)}, bf16[8,192,384]{2,1,0:T(8,128)(2,1)}, u32[]{:S(2)}, u32[]{:S(2)}) collective-permute-start(bf16[8,192,384]{2,1,0:T(8,128)(2,1)} %get-tuple-element.1075), channel_id=1, source_target_pairs={{0,1},{1,0},{2,3},{3,2},{4,5},{5,4},{6,7},{7,6},{8,9},{9,8},{10,11... | collective-permute-start | bytes 3538952 | tf_op jit(solution)/shard_map/ppermute | solution.py:29
  273.5 12.9 %collective-permute-start.33 = (bf16[79872]{0:T(1024)(128)(2,1)}, bf16[79872]{0:T(1024)(128)(2,1)}, u32[]{:S(2)}, u32[]{:S(2)}) collective-permute-start(bf16[79872]{0:T(1024)(128)(2,1)} %add_convert_fusion.16), channel_id=1, source_target_pairs={{0,16},{4,20},{8,24},{12,28},{16,0},{20,4},{24,8},{28,12},{1,17},{... | collective-permute-start | bytes 479240 | tf_op jit(solution)/shard_map/ppermute | solution.py:29
  286.4 26.1 %collective-permute-start.27 = (bf16[2,4,196,192]{2,3,1,0:T(8,128)(2,1)}, bf16[2,4,196,192]{2,3,1,0:T(8,128)(2,1)}, u32[]{:S(2)}, u32[]{:S(2)}) collective-permute-start(bf16[2,4,196,192]{2,3,1,0:T(8,128)(2,1)} %copy.478), channel_id=1, source_target_pairs={{0,2},{1,3},{2,0},{3,1},{4,6},{5,7},{6,4},{7,5},{8,10},{9,11},{10,... | collective-permute-start | bytes 1806344 | tf_op jit(solution)/shard_map/ppermute | solution.py:29
  296.2 27.1 %collective-permute-start.28 = (bf16[2,4,196,192]{2,3,1,0:T(8,128)(2,1)}, bf16[2,4,196,192]{2,3,1,0:T(8,128)(2,1)}, u32[]{:S(2)}, u32[]{:S(2)}) collective-permute-start(bf16[2,4,196,192]{2,3,1,0:T(8,128)(2,1)} %copy.479), channel_id=1, source_target_pairs={{0,3},{1,2},{2,1},{3,0},{4,7},{5,6},{6,5},{7,4},{8,11},{9,10},{10,... | collective-permute-start | bytes 1806344 | tf_op jit(solution)/shard_map/ppermute | solution.py:29
  300.7 32.5 %collective-permute-start.43 = (bf16[2,2,96,768]{3,2,1,0:T(8,128)(2,1)}, bf16[2,2,96,768]{3,2,1,0:T(8,128)(2,1)}, u32[]{:S(2)}, u32[]{:S(2)}) collective-permute-start(bf16[2,2,96,768]{3,2,1,0:T(8,128)(2,1)} %get-tuple-element.1061), channel_id=1, source_target_pairs={{0,8},{4,12},{8,0},{12,4},{16,24},{20,28},{24,16},{28,20},{1,9},{5... | collective-permute-start | bytes 1769480 | tf_op jit(solution)/shard_map/ppermute | solution.py:29
  305.3 29.6 %collective-permute-start.47 = (bf16[2,2,96,768]{3,2,1,0:T(8,128)(2,1)}, bf16[2,2,96,768]{3,2,1,0:T(8,128)(2,1)}, u32[]{:S(2)}, u32[]{:S(2)}) collective-permute-start(bf16[2,2,96,768]{3,2,1,0:T(8,128)(2,1)} %get-tuple-element.1065), channel_id=1, source_target_pairs={{0,4},{4,0},{8,12},{12,8},{16,20},{20,16},{24,28},{28,24},{1,5},{5... | collective-permute-start | bytes 1769480 | tf_op jit(solution)/shard_map/ppermute | solution.py:29
  308.4 29.9 %collective-permute-start.35 = (bf16[2,2,192,384]{3,2,1,0:T(8,128)(2,1)}, bf16[2,2,192,384]{3,2,1,0:T(8,128)(2,1)}, u32[]{:S(2)}, u32[]{:S(2)}) collective-permute-start(bf16[2,2,192,384]{3,2,1,0:T(8,128)(2,1)} %get-tuple-element.1069), channel_id=1, source_target_pairs={{0,4},{4,0},{8,12},{12,8},{16,20},{20,16},{24,28},{28,24},{1,5},{5... | collective-permute-start | bytes 1769480 | tf_op jit(solution)/shard_map/ppermute | solution.py:29
  312.5 34.5 %collective-permute-start.39 = (bf16[2,2,192,384]{3,2,1,0:T(8,128)(2,1)}, bf16[2,2,192,384]{3,2,1,0:T(8,128)(2,1)S(1)}, u32[]{:S(2)}, u32[]{:S(2)}) collective-permute-start(bf16[2,2,192,384]{3,2,1,0:T(8,128)(2,1)} %get-tuple-element.1073), channel_id=1, source_target_pairs={{0,4},{4,0},{8,12},{12,8},{16,20},{20,16},{24,28},{28,24},{1,5},{5... | collective-permute-start | bytes 1769480 | tf_op jit(solution)/shard_map/ppermute | solution.py:29
  334.5 17.8 %collective-permute-start.44 = (bf16[2,96,768]{2,1,0:T(8,128)(2,1)S(1)}, bf16[2,96,768]{2,1,0:T(8,128)(2,1)S(1)}, u32[]{:S(2)}, u32[]{:S(2)}) collective-permute-start(bf16[2,96,768]{2,1,0:T(8,128)(2,1)S(1)} %get-tuple-element.1079), channel_id=1, source_target_pairs={{0,4},{4,0},{8,12},{12,8},{16,20},{20,16},{24,28},{28,24},{1,5},{5... | collective-permute-start | bytes 884744 | tf_op jit(solution)/shard_map/ppermute | solution.py:29
  336.2 19.1 %collective-permute-start.48 = (bf16[2,96,768]{2,1,0:T(8,128)(2,1)S(1)}, bf16[2,96,768]{2,1,0:T(8,128)(2,1)S(1)}, u32[]{:S(2)}, u32[]{:S(2)}) collective-permute-start(bf16[2,96,768]{2,1,0:T(8,128)(2,1)S(1)} %get-tuple-element.1081), channel_id=1, source_target_pairs={{0,8},{4,12},{8,0},{12,4},{16,24},{20,28},{24,16},{28,20},{1,9},{5... | collective-permute-start | bytes 884744 | tf_op jit(solution)/shard_map/ppermute | solution.py:29
  339.6 15.9 %collective-permute-start.36 = (bf16[2,192,384]{2,1,0:T(8,128)(2,1)S(1)}, bf16[2,192,384]{2,1,0:T(8,128)(2,1)S(1)}, u32[]{:S(2)}, u32[]{:S(2)}) collective-permute-start(bf16[2,192,384]{2,1,0:T(8,128)(2,1)S(1)} %get-tuple-element.1083), channel_id=1, source_target_pairs={{0,8},{4,12},{8,0},{12,4},{16,24},{20,28},{24,16},{28,20},{1,9},{5... | collective-permute-start | bytes 884744 | tf_op jit(solution)/shard_map/ppermute | solution.py:29
  347.2 15.9 %collective-permute-start.40 = (bf16[2,192,384]{2,1,0:T(8,128)(2,1)S(1)}, bf16[2,192,384]{2,1,0:T(8,128)(2,1)S(1)}, u32[]{:S(2)}, u32[]{:S(2)}) collective-permute-start(bf16[2,192,384]{2,1,0:T(8,128)(2,1)S(1)} %get-tuple-element.1085), channel_id=1, source_target_pairs={{0,8},{4,12},{8,0},{12,4},{16,24},{20,28},{24,16},{28,20},{1,9},{5... | collective-permute-start | bytes 884744 | tf_op jit(solution)/shard_map/ppermute | solution.py:29
  352.3 11.7 %collective-permute-start.45 = (bf16[96,768]{1,0:T(8,128)(2,1)S(1)}, bf16[96,768]{1,0:T(8,128)(2,1)S(1)}, u32[]{:S(2)}, u32[]{:S(2)}) collective-permute-start(bf16[96,768]{1,0:T(8,128)(2,1)S(1)} %fusion.37), channel_id=1, source_target_pairs={{0,16},{4,20},{8,24},{12,28},{16,0},{20,4},{24,8},{28,12},{1,17},{... | collective-permute-start | bytes 442376 | tf_op jit(solution)/shard_map/ppermute | solution.py:29
  355.4 20.4 %collective-permute-start.49 = (bf16[96,768]{1,0:T(8,128)(2,1)S(1)}, bf16[96,768]{1,0:T(8,128)(2,1)S(1)}, u32[]{:S(2)}, u32[]{:S(2)}) collective-permute-start(bf16[96,768]{1,0:T(8,128)(2,1)S(1)} %fusion.39), channel_id=1, source_target_pairs={{0,16},{4,20},{8,24},{12,28},{16,0},{20,4},{24,8},{28,12},{1,17},{... | collective-permute-start | bytes 442376 | tf_op jit(solution)/shard_map/ppermute | solution.py:29
  355.5 23.4 %collective-permute-start.37 = (bf16[192,384]{1,0:T(8,128)(2,1)S(1)}, bf16[192,384]{1,0:T(8,128)(2,1)S(1)}, u32[]{:S(2)}, u32[]{:S(2)}) collective-permute-start(bf16[192,384]{1,0:T(8,128)(2,1)S(1)} %fusion.33), channel_id=1, source_target_pairs={{0,16},{4,20},{8,24},{12,28},{16,0},{20,4},{24,8},{28,12},{1,17},{... | collective-permute-start | bytes 442376 | tf_op jit(solution)/shard_map/ppermute | solution.py:29
  363.2 17.8 %collective-permute-start.41 = (bf16[192,384]{1,0:T(8,128)(2,1)S(1)}, bf16[192,384]{1,0:T(8,128)(2,1)S(1)}, u32[]{:S(2)}, u32[]{:S(2)}) collective-permute-start(bf16[192,384]{1,0:T(8,128)(2,1)S(1)} %fusion.35), channel_id=1, source_target_pairs={{0,16},{4,20},{8,24},{12,28},{16,0},{20,4},{24,8},{28,12},{1,17},{... | collective-permute-start | bytes 442376 | tf_op jit(solution)/shard_map/ppermute | solution.py:29
  (40 other events, 257.4 us)
